TPU v7x, 128 devices: a whole 4x4x4 slice. The times are simulated.
128 devices in a mesh: blk: 32 (over z, x, core), grp: 4 (over y).
Axes of the slice: x: 4, y: 4, z: 4, core: 2. Of those that a mesh axis runs over, the one named last changes fastest.
Arguments:
- image_emb: float32 [16384, 1152], P(('blk', 'grp')), may hold values from -0.18 to 0.18
- text_emb: float32 [16384, 1152], P(('blk', 'grp')), may hold values from -0.18 to 0.18
- logit_scale: float32 [1], replicated, may hold values from 6 to 12
- logit_bias: float32 [1], replicated, may hold values from -5 to -3
- pos_image: int32 [16384, 4], P(('blk', 'grp')), may hold values from 0 to 16383, as said below
- pos_count: int32 [16384], P(('blk', 'grp')), may hold values from 1 to 4, as said below
- image_row: int32 [16384], P(('blk', 'grp')), may hold values from 0 to 16383, as said below
Outputs:
- grad_image: float32 [16384, 1152], P(('blk', 'grp'))
- grad_text: float32 [16384, 1152], P(('blk', 'grp'))
Inputs may be any that keep to these rules, and one draw needn't show every extreme that they name: `pos_image`: only the first pos_count entries of a row count; all 4 entries of a row are distinct ids of the caption's own group: a caption in rows g * 512 to (g + 1) * 512 - 1 names ids in that same range. `pos_count`: some caption has 4 positives and some has one. `image_row`: A permutation that maps the ids of each group of 512 onto the rows of the same group.
All inputs are finite; a program needn't handle non-finite values.
Results may differ from a plain program's by a relative error of at most 0.00014.
Values sent between devices are 32-bit elements; how exact they have to be, the bound alone decides.
A program may use at most 128 MiB of HBM per device.

v0:
```python
import jax
import jax.numpy as jnp
from jax import lax
from jax.sharding import PartitionSpec as P


def passed_along(value, axis, steps):
    count = lax.axis_size(axis)
    pairs = [(source, (source + steps) % count) for source in range(count)]
    return lax.ppermute(value, axis, pairs)


def normalize(values):
    norms = jnp.sqrt(jnp.sum(values * values, axis=1, keepdims=True) + 1e-06)
    return (values / norms, norms)


def product(left, right):
    return jnp.dot(left, right, precision=lax.Precision.HIGHEST, preferred_element_type=jnp.float32)


def unproject(grad_unit, unit, norms):
    return (grad_unit - unit * jnp.sum(unit * grad_unit, axis=1, keepdims=True)) / norms


def pair_terms(unit_img, captions, temper, offset):
    sigmas = jax.nn.sigmoid(temper * product(unit_img, captions.T) + offset)
    return (temper * product(sigmas, captions), temper * product(sigmas.T, unit_img))


def run_cycle(advance, carry, steps):
    turns = min(steps, 16)
    inner = steps // turns

    def turn(counter, state):
        for repeat in range(inner):
            state = advance(state)
        return state

    return lax.fori_loop(0, turns, turn, carry)


def cycle_column(unit_img, unit_txt, temper, offset):

    def advance(carry):
        state, img_acc = carry
        img_part, txt_part = pair_terms(unit_img, state[0], temper, offset)
        moved = passed_along(jnp.stack([state[0], state[1] + txt_part]), "blk", 1)
        return (moved, img_acc + img_part)

    start = (jnp.stack([unit_txt, jnp.zeros_like(unit_txt)]), jnp.zeros_like(unit_img))
    state, img_acc = run_cycle(advance, start, lax.axis_size("blk"))
    return (img_acc, state[1])


def body(image_emb, text_emb, logit_scale, logit_bias, pos_image, pos_count, image_row):
    unit_img, img_norm = normalize(image_emb)
    unit_txt, txt_norm = normalize(text_emb)
    temper = logit_scale[0]
    offset = logit_bias[0]
    rows = image_emb.shape[0]
    groups = lax.axis_size("grp")
    listed = pos_image.shape[1]
    device = lax.axis_index("blk") * groups + lax.axis_index("grp")
    group_base = lax.axis_index("blk") * rows * groups
    img_acc, txt_acc = cycle_column(unit_img, unit_txt, temper, offset)
    block = lax.all_gather(unit_txt, "grp", axis=0, tiled=True)
    lists, counts, id_rows = (
        lax.all_gather(pos_image, "grp", axis=0, tiled=True),
        lax.all_gather(pos_count, "grp", axis=0, tiled=True),
        lax.all_gather(image_row, "grp", axis=0, tiled=True),
    )
    target = jnp.take(id_rows, lists - group_base, axis=0)
    valid = jnp.arange(listed, dtype=jnp.int32)[None, :] < counts[:, None]
    mine = target - device * rows
    hits = valid[:, :, None] & (
        mine[:, :, None] == jnp.arange(rows, dtype=jnp.int32)[None, None, :]
    )
    marks = jnp.sum(hits.astype(jnp.float32), axis=1)
    same_column = (jnp.arange(block.shape[0], dtype=jnp.int32) // rows == lax.axis_index("grp"))[
        :, None
    ]
    pair_logit = temper * product(block, unit_img.T) + offset
    coef = marks * jnp.where(same_column, -1.0, jax.nn.sigmoid(pair_logit) - 1.0)
    img_acc = img_acc + temper * product(coef.T, block)
    group_extra = temper * product(coef, unit_img)
    txt_total = txt_acc + lax.psum_scatter(group_extra, "grp", scatter_dimension=0, tiled=True)
    return (unproject(img_acc, unit_img, img_norm), unproject(txt_total, unit_txt, txt_norm))


def solution(mesh):
    return jax.shard_map(
        body,
        mesh=mesh,
        in_specs=(
            P(("blk", "grp"), None),
            P(("blk", "grp"), None),
            P(),
            P(),
            P(("blk", "grp"), None),
            P(("blk", "grp")),
            P(("blk", "grp")),
        ),
        out_specs=(P(("blk", "grp"), None), P(("blk", "grp"), None)),
        check_vma=False,
    )
```

profile of v0, /device:TPU:0, one launch (start us, length us, event | category | flops | bytes accessed | tf_op | source)
XLA Modules:
  0.0 856.9 jit_solution(4867768452492056072)
XLA Ops:
  10.5 11.3 %all_gather.13 = s32[512,4]{0,1:T(4,128)S(1)} all-gather(s32[128,4]{0,1:T(4,128)S(1)} %copy-done.9), channel_id=1, replica_groups=mesh['blk'=32,'grp'=4] {'grp'}, dimensions={0}, use_global_device_ids=true | all-gather | bytes 10240 | tf_op jit(solution)/shard_map/all_gather | solution.py:69
  22.2 8.8 %all-gather.1 = s32[4,1,128]{2,1,0:T(1,128)S(1)} all-gather(s32[1,1,128]{2,1,0:T(1,128)S(1)} %bitcast.88), channel_id=1, replica_groups=mesh['blk'=32,'grp'=4] {'grp'}, dimensions={0}, use_global_device_ids=true | all-gather | bytes 2560 | tf_op jit(solution)/shard_map/all_gather | solution.py:71
  31.0 13.2 %gather_fusion = s32[2048]{0:T(1024)S(1)} fusion(s32[512]{0:T(512)S(1)} %bitcast.86, s32[2048]{0:T(1024)S(1)} %broadcast_clamp_fusion), kind=kCustom, calls=%fused_computation | custom fusion | bytes 24576 | tf_op jit(solution)/shard_map/jit(_take)/gather | solution.py:73
  46.7 7.0 all-gather
  54.8 3.8 fusion.32
  59.3 3.4 convolution_multiply_fusion.6
  62.7 780.5 %while.13 = (s32[]{:T(128)}, f32[2,128,1152]{2,1,0:T(8,128)S(1)}, f32[128,1152]{1,0:T(8,128)S(1)}, f32[]{:T(128)}, f32[128,1152]{1,0:T(8,128)S(1)}, /*index=5*/f32[]{:T(128)}, s32[]{:T(128)}, s32[]{:T(128)}) while((s32[]{:T(128)}, f32[2,128,1152]{2,1,0:T(8,128)S(1)}, f32[128,1152]{1,0:T(8,128)S(1)}, f32[]{:T(128)}, ...), condition=%wide.region_3.0_spmd.clone, body=%wide.region_2.0_spmd.clone.sunk | while | flops 1361035264 | bytes 29491496 | solution.py:40
  66.9 18.9 %collective-permute-done = f32[2,128,1152]{2,1,0:T(8,128)S(1)} collective-permute-done((f32[2,128,1152]{2,1,0:T(8,128)S(1)}, f32[2,128,1152]{2,1,0:T(8,128)S(1)}, u32[]{:S(2)}, u32[]{:S(2)}) %collective-permute-start) | collective-permute-done | bytes 1179680 | tf_op jit(solution)/shard_map/while/body/eval_jaxpr/ppermute | solution.py:10
  91.0 2.2 fusion.87
  94.5 15.8 %collective-permute-done.1 = f32[2,128,1152]{2,1,0:T(8,128)} collective-permute-done((f32[2,128,1152]{2,1,0:T(8,128)}, f32[2,128,1152]{2,1,0:T(8,128)}, u32[]{:S(2)}, u32[]{:S(2)}) %collective-permute-start.1) | collective-permute-done | bytes 1179680 | tf_op jit(solution)/shard_map/while/body/eval_jaxpr/ppermute | solution.py:10
  111.5 2.1 fusion.83
  115.7 18.9 %collective-permute-done = f32[2,128,1152]{2,1,0:T(8,128)S(1)} collective-permute-done((f32[2,128,1152]{2,1,0:T(8,128)S(1)}, f32[2,128,1152]{2,1,0:T(8,128)S(1)}, u32[]{:S(2)}, u32[]{:S(2)}) %collective-permute-start) | collective-permute-done | bytes 1179680 | tf_op jit(solution)/shard_map/while/body/eval_jaxpr/ppermute | solution.py:10
  139.7 2.2 fusion.87
  143.3 15.8 %collective-permute-done.1 = f32[2,128,1152]{2,1,0:T(8,128)} collective-permute-done((f32[2,128,1152]{2,1,0:T(8,128)}, f32[2,128,1152]{2,1,0:T(8,128)}, u32[]{:S(2)}, u32[]{:S(2)}) %collective-permute-start.1) | collective-permute-done | bytes 1179680 | tf_op jit(solution)/shard_map/while/body/eval_jaxpr/ppermute | solution.py:10
  160.3 2.1 fusion.83
  164.5 18.9 %collective-permute-done = f32[2,128,1152]{2,1,0:T(8,128)S(1)} collective-permute-done((f32[2,128,1152]{2,1,0:T(8,128)S(1)}, f32[2,128,1152]{2,1,0:T(8,128)S(1)}, u32[]{:S(2)}, u32[]{:S(2)}) %collective-permute-start) | collective-permute-done | bytes 1179680 | tf_op jit(solution)/shard_map/while/body/eval_jaxpr/ppermute | solution.py:10
  188.5 2.2 fusion.87
  192.0 15.8 %collective-permute-done.1 = f32[2,128,1152]{2,1,0:T(8,128)} collective-permute-done((f32[2,128,1152]{2,1,0:T(8,128)}, f32[2,128,1152]{2,1,0:T(8,128)}, u32[]{:S(2)}, u32[]{:S(2)}) %collective-permute-start.1) | collective-permute-done | bytes 1179680 | tf_op jit(solution)/shard_map/while/body/eval_jaxpr/ppermute | solution.py:10
  209.1 2.1 fusion.83
  213.3 18.9 %collective-permute-done = f32[2,128,1152]{2,1,0:T(8,128)S(1)} collective-permute-done((f32[2,128,1152]{2,1,0:T(8,128)S(1)}, f32[2,128,1152]{2,1,0:T(8,128)S(1)}, u32[]{:S(2)}, u32[]{:S(2)}) %collective-permute-start) | collective-permute-done | bytes 1179680 | tf_op jit(solution)/shard_map/while/body/eval_jaxpr/ppermute | solution.py:10
  237.3 2.2 fusion.87
  240.8 15.8 %collective-permute-done.1 = f32[2,128,1152]{2,1,0:T(8,128)} collective-permute-done((f32[2,128,1152]{2,1,0:T(8,128)}, f32[2,128,1152]{2,1,0:T(8,128)}, u32[]{:S(2)}, u32[]{:S(2)}) %collective-permute-start.1) | collective-permute-done | bytes 1179680 | tf_op jit(solution)/shard_map/while/body/eval_jaxpr/ppermute | solution.py:10
  257.9 2.1 fusion.83
  262.1 18.9 %collective-permute-done = f32[2,128,1152]{2,1,0:T(8,128)S(1)} collective-permute-done((f32[2,128,1152]{2,1,0:T(8,128)S(1)}, f32[2,128,1152]{2,1,0:T(8,128)S(1)}, u32[]{:S(2)}, u32[]{:S(2)}) %collective-permute-start) | collective-permute-done | bytes 1179680 | tf_op jit(solution)/shard_map/while/body/eval_jaxpr/ppermute | solution.py:10
  286.1 2.2 fusion.87
  289.6 15.8 %collective-permute-done.1 = f32[2,128,1152]{2,1,0:T(8,128)} collective-permute-done((f32[2,128,1152]{2,1,0:T(8,128)}, f32[2,128,1152]{2,1,0:T(8,128)}, u32[]{:S(2)}, u32[]{:S(2)}) %collective-permute-start.1) | collective-permute-done | bytes 1179680 | tf_op jit(solution)/shard_map/while/body/eval_jaxpr/ppermute | solution.py:10
  306.7 2.1 fusion.83
  310.9 18.9 %collective-permute-done = f32[2,128,1152]{2,1,0:T(8,128)S(1)} collective-permute-done((f32[2,128,1152]{2,1,0:T(8,128)S(1)}, f32[2,128,1152]{2,1,0:T(8,128)S(1)}, u32[]{:S(2)}, u32[]{:S(2)}) %collective-permute-start) | collective-permute-done | bytes 1179680 | tf_op jit(solution)/shard_map/while/body/eval_jaxpr/ppermute | solution.py:10
  334.9 2.2 fusion.87
  338.4 15.8 %collective-permute-done.1 = f32[2,128,1152]{2,1,0:T(8,128)} collective-permute-done((f32[2,128,1152]{2,1,0:T(8,128)}, f32[2,128,1152]{2,1,0:T(8,128)}, u32[]{:S(2)}, u32[]{:S(2)}) %collective-permute-start.1) | collective-permute-done | bytes 1179680 | tf_op jit(solution)/shard_map/while/body/eval_jaxpr/ppermute | solution.py:10
  355.5 2.1 fusion.83
  359.6 18.9 %collective-permute-done = f32[2,128,1152]{2,1,0:T(8,128)S(1)} collective-permute-done((f32[2,128,1152]{2,1,0:T(8,128)S(1)}, f32[2,128,1152]{2,1,0:T(8,128)S(1)}, u32[]{:S(2)}, u32[]{:S(2)}) %collective-permute-start) | collective-permute-done | bytes 1179680 | tf_op jit(solution)/shard_map/while/body/eval_jaxpr/ppermute | solution.py:10
  383.7 2.2 fusion.87
  387.2 15.8 %collective-permute-done.1 = f32[2,128,1152]{2,1,0:T(8,128)} collective-permute-done((f32[2,128,1152]{2,1,0:T(8,128)}, f32[2,128,1152]{2,1,0:T(8,128)}, u32[]{:S(2)}, u32[]{:S(2)}) %collective-permute-start.1) | collective-permute-done | bytes 1179680 | tf_op jit(solution)/shard_map/while/body/eval_jaxpr/ppermute | solution.py:10
  404.2 2.1 fusion.83
  408.4 18.9 %collective-permute-done = f32[2,128,1152]{2,1,0:T(8,128)S(1)} collective-permute-done((f32[2,128,1152]{2,1,0:T(8,128)S(1)}, f32[2,128,1152]{2,1,0:T(8,128)S(1)}, u32[]{:S(2)}, u32[]{:S(2)}) %collective-permute-start) | collective-permute-done | bytes 1179680 | tf_op jit(solution)/shard_map/while/body/eval_jaxpr/ppermute | solution.py:10
  432.4 2.2 fusion.87
  435.9 15.8 %collective-permute-done.1 = f32[2,128,1152]{2,1,0:T(8,128)} collective-permute-done((f32[2,128,1152]{2,1,0:T(8,128)}, f32[2,128,1152]{2,1,0:T(8,128)}, u32[]{:S(2)}, u32[]{:S(2)}) %collective-permute-start.1) | collective-permute-done | bytes 1179680 | tf_op jit(solution)/shard_map/while/body/eval_jaxpr/ppermute | solution.py:10
  453.0 2.1 fusion.83
  457.2 18.9 %collective-permute-done = f32[2,128,1152]{2,1,0:T(8,128)S(1)} collective-permute-done((f32[2,128,1152]{2,1,0:T(8,128)S(1)}, f32[2,128,1152]{2,1,0:T(8,128)S(1)}, u32[]{:S(2)}, u32[]{:S(2)}) %collective-permute-start) | collective-permute-done | bytes 1179680 | tf_op jit(solution)/shard_map/while/body/eval_jaxpr/ppermute | solution.py:10
  481.2 2.2 fusion.87
  484.7 15.8 %collective-permute-done.1 = f32[2,128,1152]{2,1,0:T(8,128)} collective-permute-done((f32[2,128,1152]{2,1,0:T(8,128)}, f32[2,128,1152]{2,1,0:T(8,128)}, u32[]{:S(2)}, u32[]{:S(2)}) %collective-permute-start.1) | collective-permute-done | bytes 1179680 | tf_op jit(solution)/shard_map/while/body/eval_jaxpr/ppermute | solution.py:10
  506.0 18.9 %collective-permute-done = f32[2,128,1152]{2,1,0:T(8,128)S(1)} collective-permute-done((f32[2,128,1152]{2,1,0:T(8,128)S(1)}, f32[2,128,1152]{2,1,0:T(8,128)S(1)}, u32[]{:S(2)}, u32[]{:S(2)}) %collective-permute-start) | collective-permute-done | bytes 1179680 | tf_op jit(solution)/shard_map/while/body/eval_jaxpr/ppermute | solution.py:10
  530.0 2.2 fusion.87
  533.5 15.8 %collective-permute-done.1 = f32[2,128,1152]{2,1,0:T(8,128)} collective-permute-done((f32[2,128,1152]{2,1,0:T(8,128)}, f32[2,128,1152]{2,1,0:T(8,128)}, u32[]{:S(2)}, u32[]{:S(2)}) %collective-permute-start.1) | collective-permute-done | bytes 1179680 | tf_op jit(solution)/shard_map/while/body/eval_jaxpr/ppermute | solution.py:10
  554.8 18.9 %collective-permute-done = f32[2,128,1152]{2,1,0:T(8,128)S(1)} collective-permute-done((f32[2,128,1152]{2,1,0:T(8,128)S(1)}, f32[2,128,1152]{2,1,0:T(8,128)S(1)}, u32[]{:S(2)}, u32[]{:S(2)}) %collective-permute-start) | collective-permute-done | bytes 1179680 | tf_op jit(solution)/shard_map/while/body/eval_jaxpr/ppermute | solution.py:10
  578.8 2.2 fusion.87
  582.3 15.8 %collective-permute-done.1 = f32[2,128,1152]{2,1,0:T(8,128)} collective-permute-done((f32[2,128,1152]{2,1,0:T(8,128)}, f32[2,128,1152]{2,1,0:T(8,128)}, u32[]{:S(2)}, u32[]{:S(2)}) %collective-permute-start.1) | collective-permute-done | bytes 1179680 | tf_op jit(solution)/shard_map/while/body/eval_jaxpr/ppermute | solution.py:10
  603.6 18.9 %collective-permute-done = f32[2,128,1152]{2,1,0:T(8,128)S(1)} collective-permute-done((f32[2,128,1152]{2,1,0:T(8,128)S(1)}, f32[2,128,1152]{2,1,0:T(8,128)S(1)}, u32[]{:S(2)}, u32[]{:S(2)}) %collective-permute-start) | collective-permute-done | bytes 1179680 | tf_op jit(solution)/shard_map/while/body/eval_jaxpr/ppermute | solution.py:10
  627.6 2.2 fusion.87
  631.1 15.8 %collective-permute-done.1 = f32[2,128,1152]{2,1,0:T(8,128)} collective-permute-done((f32[2,128,1152]{2,1,0:T(8,128)}, f32[2,128,1152]{2,1,0:T(8,128)}, u32[]{:S(2)}, u32[]{:S(2)}) %collective-permute-start.1) | collective-permute-done | bytes 1179680 | tf_op jit(solution)/shard_map/while/body/eval_jaxpr/ppermute | solution.py:10
  652.3 18.9 %collective-permute-done = f32[2,128,1152]{2,1,0:T(8,128)S(1)} collective-permute-done((f32[2,128,1152]{2,1,0:T(8,128)S(1)}, f32[2,128,1152]{2,1,0:T(8,128)S(1)}, u32[]{:S(2)}, u32[]{:S(2)}) %collective-permute-start) | collective-permute-done | bytes 1179680 | tf_op jit(solution)/shard_map/while/body/eval_jaxpr/ppermute | solution.py:10
  676.4 2.2 fusion.87
  679.9 15.8 %collective-permute-done.1 = f32[2,128,1152]{2,1,0:T(8,128)} collective-permute-done((f32[2,128,1152]{2,1,0:T(8,128)}, f32[2,128,1152]{2,1,0:T(8,128)}, u32[]{:S(2)}, u32[]{:S(2)}) %collective-permute-start.1) | collective-permute-done | bytes 1179680 | tf_op jit(solution)/shard_map/while/body/eval_jaxpr/ppermute | solution.py:10
  701.1 18.9 %collective-permute-done = f32[2,128,1152]{2,1,0:T(8,128)S(1)} collective-permute-done((f32[2,128,1152]{2,1,0:T(8,128)S(1)}, f32[2,128,1152]{2,1,0:T(8,128)S(1)}, u32[]{:S(2)}, u32[]{:S(2)}) %collective-permute-start) | collective-permute-done | bytes 1179680 | tf_op jit(solution)/shard_map/while/body/eval_jaxpr/ppermute | solution.py:10
  725.1 2.2 fusion.87
  728.6 15.8 %collective-permute-done.1 = f32[2,128,1152]{2,1,0:T(8,128)} collective-permute-done((f32[2,128,1152]{2,1,0:T(8,128)}, f32[2,128,1152]{2,1,0:T(8,128)}, u32[]{:S(2)}, u32[]{:S(2)}) %collective-permute-start.1) | collective-permute-done | bytes 1179680 | tf_op jit(solution)/shard_map/while/body/eval_jaxpr/ppermute | solution.py:10
  749.9 18.9 %collective-permute-done = f32[2,128,1152]{2,1,0:T(8,128)S(1)} collective-permute-done((f32[2,128,1152]{2,1,0:T(8,128)S(1)}, f32[2,128,1152]{2,1,0:T(8,128)S(1)}, u32[]{:S(2)}, u32[]{:S(2)}) %collective-permute-start) | collective-permute-done | bytes 1179680 | tf_op jit(solution)/shard_map/while/body/eval_jaxpr/ppermute | solution.py:10
  773.9 2.2 fusion.87
  777.4 15.8 %collective-permute-done.1 = f32[2,128,1152]{2,1,0:T(8,128)} collective-permute-done((f32[2,128,1152]{2,1,0:T(8,128)}, f32[2,128,1152]{2,1,0:T(8,128)}, u32[]{:S(2)}, u32[]{:S(2)}) %collective-permute-start.1) | collective-permute-done | bytes 1179680 | tf_op jit(solution)/shard_map/while/body/eval_jaxpr/ppermute | solution.py:10
  798.7 18.9 %collective-permute-done = f32[2,128,1152]{2,1,0:T(8,128)S(1)} collective-permute-done((f32[2,128,1152]{2,1,0:T(8,128)S(1)}, f32[2,128,1152]{2,1,0:T(8,128)S(1)}, u32[]{:S(2)}, u32[]{:S(2)}) %collective-permute-start) | collective-permute-done | bytes 1179680 | tf_op jit(solution)/shard_map/while/body/eval_jaxpr/ppermute | solution.py:10
  822.7 2.2 fusion.87
  826.2 15.8 %collective-permute-done.1 = f32[2,128,1152]{2,1,0:T(8,128)} collective-permute-done((f32[2,128,1152]{2,1,0:T(8,128)}, f32[2,128,1152]{2,1,0:T(8,128)}, u32[]{:S(2)}, u32[]{:S(2)}) %collective-permute-start.1) | collective-permute-done | bytes 1179680 | tf_op jit(solution)/shard_map/while/body/eval_jaxpr/ppermute | solution.py:10
  843.2 3.4 multiply_reduce_fusion.1
  (326 shorter events, 182.8 us)
Async XLA Ops:
  7.2 3.3 copy-start.9
  7.2 47.6 %all-gather.4.cloned.1.call-start = ((), (), s32[]{:S(2)}) async-start(), calls=%async_computation.1 | async-start | bytes 2949120 | tf_op jit(solution)/shard_map/all_gather | solution.py:67
  8.4 13.8 %copy-start.10 = (s32[128]{0:T(128)S(1)}, s32[128]{0:T(128)}, u32[]{:S(2)}) copy-start(s32[128]{0:T(128)} %param.15) | copy-start | bytes 1540
  10.4 837.2 %reduce-scatter.2.cloned.1.call-start = ((), (), s32[]{:S(2)}) async-start(), calls=%async_computation.2 | async-start | bytes 2949120 | tf_op jit(solution)/shard_map/reduce_scatter | solution.py:87
  31.0 14.9 %copy-start.3 = (f32[128,1152]{1,0:T(8,128)S(1)}, f32[128,1152]{1,0:T(8,128)}, u32[]{:S(2)}) copy-start(f32[128,1152]{1,0:T(8,128)} %param.10) | copy-start | bytes 1769476
  46.0 0.7 copy-start.11
  46.0 7.7 copy-start.5
  58.6 0.7 copy-start.8
  64.8 0.6 copy-start
  66.9 19.0 %collective-permute-start = (f32[2,128,1152]{2,1,0:T(8,128)S(1)}, f32[2,128,1152]{2,1,0:T(8,128)S(1)}, u32[]{:S(2)}, u32[]{:S(2)}) collective-permute-start(f32[2,128,1152]{2,1,0:T(8,128)S(1)} %pad_maximum_fusion.4), channel_id=1, source_target_pairs={{0,4},{4,8},{8,12},{12,16},{16,20},{20,24},{24,28},{28,32},{32,36}... | collective-permute-start | bytes 3538952 | tf_op jit(solution)/shard_map/while/body/eval_jaxpr/ppermute | solution.py:10
  91.0 19.3 %collective-permute-start.1 = (f32[2,128,1152]{2,1,0:T(8,128)}, f32[2,128,1152]{2,1,0:T(8,128)}, u32[]{:S(2)}, u32[]{:S(2)}) collective-permute-start(f32[2,128,1152]{2,1,0:T(8,128)} %pad_maximum_fusion.5), channel_id=1, source_target_pairs={{0,4},{4,8},{8,12},{12,16},{16,20},{20,24},{24,28},{28,32},{32,36}... | collective-permute-start | bytes 3538952 | tf_op jit(solution)/shard_map/while/body/eval_jaxpr/ppermute | solution.py:10
  91.0 2.2 copy-start.2
  113.6 0.6 copy-start
  115.6 19.0 %collective-permute-start = (f32[2,128,1152]{2,1,0:T(8,128)S(1)}, f32[2,128,1152]{2,1,0:T(8,128)S(1)}, u32[]{:S(2)}, u32[]{:S(2)}) collective-permute-start(f32[2,128,1152]{2,1,0:T(8,128)S(1)} %pad_maximum_fusion.4), channel_id=1, source_target_pairs={{0,4},{4,8},{8,12},{12,16},{16,20},{20,24},{24,28},{28,32},{32,36}... | collective-permute-start | bytes 3538952 | tf_op jit(solution)/shard_map/while/body/eval_jaxpr/ppermute | solution.py:10
  139.7 19.3 %collective-permute-start.1 = (f32[2,128,1152]{2,1,0:T(8,128)}, f32[2,128,1152]{2,1,0:T(8,128)}, u32[]{:S(2)}, u32[]{:S(2)}) collective-permute-start(f32[2,128,1152]{2,1,0:T(8,128)} %pad_maximum_fusion.5), channel_id=1, source_target_pairs={{0,4},{4,8},{8,12},{12,16},{16,20},{20,24},{24,28},{28,32},{32,36}... | collective-permute-start | bytes 3538952 | tf_op jit(solution)/shard_map/while/body/eval_jaxpr/ppermute | solution.py:10
  139.7 2.2 copy-start.2
  162.4 0.6 copy-start
  164.4 19.0 %collective-permute-start = (f32[2,128,1152]{2,1,0:T(8,128)S(1)}, f32[2,128,1152]{2,1,0:T(8,128)S(1)}, u32[]{:S(2)}, u32[]{:S(2)}) collective-permute-start(f32[2,128,1152]{2,1,0:T(8,128)S(1)} %pad_maximum_fusion.4), channel_id=1, source_target_pairs={{0,4},{4,8},{8,12},{12,16},{16,20},{20,24},{24,28},{28,32},{32,36}... | collective-permute-start | bytes 3538952 | tf_op jit(solution)/shard_map/while/body/eval_jaxpr/ppermute | solution.py:10
  188.5 19.3 %collective-permute-start.1 = (f32[2,128,1152]{2,1,0:T(8,128)}, f32[2,128,1152]{2,1,0:T(8,128)}, u32[]{:S(2)}, u32[]{:S(2)}) collective-permute-start(f32[2,128,1152]{2,1,0:T(8,128)} %pad_maximum_fusion.5), channel_id=1, source_target_pairs={{0,4},{4,8},{8,12},{12,16},{16,20},{20,24},{24,28},{28,32},{32,36}... | collective-permute-start | bytes 3538952 | tf_op jit(solution)/shard_map/while/body/eval_jaxpr/ppermute | solution.py:10
  188.5 2.2 copy-start.2
  213.2 19.0 %collective-permute-start = (f32[2,128,1152]{2,1,0:T(8,128)S(1)}, f32[2,128,1152]{2,1,0:T(8,128)S(1)}, u32[]{:S(2)}, u32[]{:S(2)}) collective-permute-start(f32[2,128,1152]{2,1,0:T(8,128)S(1)} %pad_maximum_fusion.4), channel_id=1, source_target_pairs={{0,4},{4,8},{8,12},{12,16},{16,20},{20,24},{24,28},{28,32},{32,36}... | collective-permute-start | bytes 3538952 | tf_op jit(solution)/shard_map/while/body/eval_jaxpr/ppermute | solution.py:10
  237.3 19.3 %collective-permute-start.1 = (f32[2,128,1152]{2,1,0:T(8,128)}, f32[2,128,1152]{2,1,0:T(8,128)}, u32[]{:S(2)}, u32[]{:S(2)}) collective-permute-start(f32[2,128,1152]{2,1,0:T(8,128)} %pad_maximum_fusion.5), channel_id=1, source_target_pairs={{0,4},{4,8},{8,12},{12,16},{16,20},{20,24},{24,28},{28,32},{32,36}... | collective-permute-start | bytes 3538952 | tf_op jit(solution)/shard_map/while/body/eval_jaxpr/ppermute | solution.py:10
  237.3 2.2 copy-start.2
  262.0 19.0 %collective-permute-start = (f32[2,128,1152]{2,1,0:T(8,128)S(1)}, f32[2,128,1152]{2,1,0:T(8,128)S(1)}, u32[]{:S(2)}, u32[]{:S(2)}) collective-permute-start(f32[2,128,1152]{2,1,0:T(8,128)S(1)} %pad_maximum_fusion.4), channel_id=1, source_target_pairs={{0,4},{4,8},{8,12},{12,16},{16,20},{20,24},{24,28},{28,32},{32,36}... | collective-permute-start | bytes 3538952 | tf_op jit(solution)/shard_map/while/body/eval_jaxpr/ppermute | solution.py:10
  286.1 19.3 %collective-permute-start.1 = (f32[2,128,1152]{2,1,0:T(8,128)}, f32[2,128,1152]{2,1,0:T(8,128)}, u32[]{:S(2)}, u32[]{:S(2)}) collective-permute-start(f32[2,128,1152]{2,1,0:T(8,128)} %pad_maximum_fusion.5), channel_id=1, source_target_pairs={{0,4},{4,8},{8,12},{12,16},{16,20},{20,24},{24,28},{28,32},{32,36}... | collective-permute-start | bytes 3538952 | tf_op jit(solution)/shard_map/while/body/eval_jaxpr/ppermute | solution.py:10
  286.1 2.2 copy-start.2
  310.8 19.0 %collective-permute-start = (f32[2,128,1152]{2,1,0:T(8,128)S(1)}, f32[2,128,1152]{2,1,0:T(8,128)S(1)}, u32[]{:S(2)}, u32[]{:S(2)}) collective-permute-start(f32[2,128,1152]{2,1,0:T(8,128)S(1)} %pad_maximum_fusion.4), channel_id=1, source_target_pairs={{0,4},{4,8},{8,12},{12,16},{16,20},{20,24},{24,28},{28,32},{32,36}... | collective-permute-start | bytes 3538952 | tf_op jit(solution)/shard_map/while/body/eval_jaxpr/ppermute | solution.py:10
  334.9 19.3 %collective-permute-start.1 = (f32[2,128,1152]{2,1,0:T(8,128)}, f32[2,128,1152]{2,1,0:T(8,128)}, u32[]{:S(2)}, u32[]{:S(2)}) collective-permute-start(f32[2,128,1152]{2,1,0:T(8,128)} %pad_maximum_fusion.5), channel_id=1, source_target_pairs={{0,4},{4,8},{8,12},{12,16},{16,20},{20,24},{24,28},{28,32},{32,36}... | collective-permute-start | bytes 3538952 | tf_op jit(solution)/shard_map/while/body/eval_jaxpr/ppermute | solution.py:10
  334.9 2.2 copy-start.2
  359.6 19.0 %collective-permute-start = (f32[2,128,1152]{2,1,0:T(8,128)S(1)}, f32[2,128,1152]{2,1,0:T(8,128)S(1)}, u32[]{:S(2)}, u32[]{:S(2)}) collective-permute-start(f32[2,128,1152]{2,1,0:T(8,128)S(1)} %pad_maximum_fusion.4), channel_id=1, source_target_pairs={{0,4},{4,8},{8,12},{12,16},{16,20},{20,24},{24,28},{28,32},{32,36}... | collective-permute-start | bytes 3538952 | tf_op jit(solution)/shard_map/while/body/eval_jaxpr/ppermute | solution.py:10
  383.7 19.3 %collective-permute-start.1 = (f32[2,128,1152]{2,1,0:T(8,128)}, f32[2,128,1152]{2,1,0:T(8,128)}, u32[]{:S(2)}, u32[]{:S(2)}) collective-permute-start(f32[2,128,1152]{2,1,0:T(8,128)} %pad_maximum_fusion.5), channel_id=1, source_target_pairs={{0,4},{4,8},{8,12},{12,16},{16,20},{20,24},{24,28},{28,32},{32,36}... | collective-permute-start | bytes 3538952 | tf_op jit(solution)/shard_map/while/body/eval_jaxpr/ppermute | solution.py:10
  383.7 2.2 copy-start.2
  408.3 19.0 %collective-permute-start = (f32[2,128,1152]{2,1,0:T(8,128)S(1)}, f32[2,128,1152]{2,1,0:T(8,128)S(1)}, u32[]{:S(2)}, u32[]{:S(2)}) collective-permute-start(f32[2,128,1152]{2,1,0:T(8,128)S(1)} %pad_maximum_fusion.4), channel_id=1, source_target_pairs={{0,4},{4,8},{8,12},{12,16},{16,20},{20,24},{24,28},{28,32},{32,36}... | collective-permute-start | bytes 3538952 | tf_op jit(solution)/shard_map/while/body/eval_jaxpr/ppermute | solution.py:10
  432.4 19.3 %collective-permute-start.1 = (f32[2,128,1152]{2,1,0:T(8,128)}, f32[2,128,1152]{2,1,0:T(8,128)}, u32[]{:S(2)}, u32[]{:S(2)}) collective-permute-start(f32[2,128,1152]{2,1,0:T(8,128)} %pad_maximum_fusion.5), channel_id=1, source_target_pairs={{0,4},{4,8},{8,12},{12,16},{16,20},{20,24},{24,28},{28,32},{32,36}... | collective-permute-start | bytes 3538952 | tf_op jit(solution)/shard_map/while/body/eval_jaxpr/ppermute | solution.py:10
  432.4 2.2 copy-start.2
  455.1 0.6 copy-start
  457.1 19.0 %collective-permute-start = (f32[2,128,1152]{2,1,0:T(8,128)S(1)}, f32[2,128,1152]{2,1,0:T(8,128)S(1)}, u32[]{:S(2)}, u32[]{:S(2)}) collective-permute-start(f32[2,128,1152]{2,1,0:T(8,128)S(1)} %pad_maximum_fusion.4), channel_id=1, source_target_pairs={{0,4},{4,8},{8,12},{12,16},{16,20},{20,24},{24,28},{28,32},{32,36}... | collective-permute-start | bytes 3538952 | tf_op jit(solution)/shard_map/while/body/eval_jaxpr/ppermute | solution.py:10
  481.2 19.3 %collective-permute-start.1 = (f32[2,128,1152]{2,1,0:T(8,128)}, f32[2,128,1152]{2,1,0:T(8,128)}, u32[]{:S(2)}, u32[]{:S(2)}) collective-permute-start(f32[2,128,1152]{2,1,0:T(8,128)} %pad_maximum_fusion.5), channel_id=1, source_target_pairs={{0,4},{4,8},{8,12},{12,16},{16,20},{20,24},{24,28},{28,32},{32,36}... | collective-permute-start | bytes 3538952 | tf_op jit(solution)/shard_map/while/body/eval_jaxpr/ppermute | solution.py:10
  481.2 2.2 copy-start.2
  503.9 0.6 copy-start
  505.9 19.0 %collective-permute-start = (f32[2,128,1152]{2,1,0:T(8,128)S(1)}, f32[2,128,1152]{2,1,0:T(8,128)S(1)}, u32[]{:S(2)}, u32[]{:S(2)}) collective-permute-start(f32[2,128,1152]{2,1,0:T(8,128)S(1)} %pad_maximum_fusion.4), channel_id=1, source_target_pairs={{0,4},{4,8},{8,12},{12,16},{16,20},{20,24},{24,28},{28,32},{32,36}... | collective-permute-start | bytes 3538952 | tf_op jit(solution)/shard_map/while/body/eval_jaxpr/ppermute | solution.py:10
  530.0 19.3 %collective-permute-start.1 = (f32[2,128,1152]{2,1,0:T(8,128)}, f32[2,128,1152]{2,1,0:T(8,128)}, u32[]{:S(2)}, u32[]{:S(2)}) collective-permute-start(f32[2,128,1152]{2,1,0:T(8,128)} %pad_maximum_fusion.5), channel_id=1, source_target_pairs={{0,4},{4,8},{8,12},{12,16},{16,20},{20,24},{24,28},{28,32},{32,36}... | collective-permute-start | bytes 3538952 | tf_op jit(solution)/shard_map/while/body/eval_jaxpr/ppermute | solution.py:10
  530.0 2.2 copy-start.2
  554.7 19.0 %collective-permute-start = (f32[2,128,1152]{2,1,0:T(8,128)S(1)}, f32[2,128,1152]{2,1,0:T(8,128)S(1)}, u32[]{:S(2)}, u32[]{:S(2)}) collective-permute-start(f32[2,128,1152]{2,1,0:T(8,128)S(1)} %pad_maximum_fusion.4), channel_id=1, source_target_pairs={{0,4},{4,8},{8,12},{12,16},{16,20},{20,24},{24,28},{28,32},{32,36}... | collective-permute-start | bytes 3538952 | tf_op jit(solution)/shard_map/while/body/eval_jaxpr/ppermute | solution.py:10
  578.8 19.3 %collective-permute-start.1 = (f32[2,128,1152]{2,1,0:T(8,128)}, f32[2,128,1152]{2,1,0:T(8,128)}, u32[]{:S(2)}, u32[]{:S(2)}) collective-permute-start(f32[2,128,1152]{2,1,0:T(8,128)} %pad_maximum_fusion.5), channel_id=1, source_target_pairs={{0,4},{4,8},{8,12},{12,16},{16,20},{20,24},{24,28},{28,32},{32,36}... | collective-permute-start | bytes 3538952 | tf_op jit(solution)/shard_map/while/body/eval_jaxpr/ppermute | solution.py:10
  578.8 2.2 copy-start.2
  603.5 19.0 %collective-permute-start = (f32[2,128,1152]{2,1,0:T(8,128)S(1)}, f32[2,128,1152]{2,1,0:T(8,128)S(1)}, u32[]{:S(2)}, u32[]{:S(2)}) collective-permute-start(f32[2,128,1152]{2,1,0:T(8,128)S(1)} %pad_maximum_fusion.4), channel_id=1, source_target_pairs={{0,4},{4,8},{8,12},{12,16},{16,20},{20,24},{24,28},{28,32},{32,36}... | collective-permute-start | bytes 3538952 | tf_op jit(solution)/shard_map/while/body/eval_jaxpr/ppermute | solution.py:10
  627.6 19.3 %collective-permute-start.1 = (f32[2,128,1152]{2,1,0:T(8,128)}, f32[2,128,1152]{2,1,0:T(8,128)}, u32[]{:S(2)}, u32[]{:S(2)}) collective-permute-start(f32[2,128,1152]{2,1,0:T(8,128)} %pad_maximum_fusion.5), channel_id=1, source_target_pairs={{0,4},{4,8},{8,12},{12,16},{16,20},{20,24},{24,28},{28,32},{32,36}... | collective-permute-start | bytes 3538952 | tf_op jit(solution)/shard_map/while/body/eval_jaxpr/ppermute | solution.py:10
  627.6 2.2 copy-start.2
  652.3 19.0 %collective-permute-start = (f32[2,128,1152]{2,1,0:T(8,128)S(1)}, f32[2,128,1152]{2,1,0:T(8,128)S(1)}, u32[]{:S(2)}, u32[]{:S(2)}) collective-permute-start(f32[2,128,1152]{2,1,0:T(8,128)S(1)} %pad_maximum_fusion.4), channel_id=1, source_target_pairs={{0,4},{4,8},{8,12},{12,16},{16,20},{20,24},{24,28},{28,32},{32,36}... | collective-permute-start | bytes 3538952 | tf_op jit(solution)/shard_map/while/body/eval_jaxpr/ppermute | solution.py:10
  676.4 19.3 %collective-permute-start.1 = (f32[2,128,1152]{2,1,0:T(8,128)}, f32[2,128,1152]{2,1,0:T(8,128)}, u32[]{:S(2)}, u32[]{:S(2)}) collective-permute-start(f32[2,128,1152]{2,1,0:T(8,128)} %pad_maximum_fusion.5), channel_id=1, source_target_pairs={{0,4},{4,8},{8,12},{12,16},{16,20},{20,24},{24,28},{28,32},{32,36}... | collective-permute-start | bytes 3538952 | tf_op jit(solution)/shard_map/while/body/eval_jaxpr/ppermute | solution.py:10
  676.4 2.2 copy-start.2
  701.0 19.0 %collective-permute-start = (f32[2,128,1152]{2,1,0:T(8,128)S(1)}, f32[2,128,1152]{2,1,0:T(8,128)S(1)}, u32[]{:S(2)}, u32[]{:S(2)}) collective-permute-start(f32[2,128,1152]{2,1,0:T(8,128)S(1)} %pad_maximum_fusion.4), channel_id=1, source_target_pairs={{0,4},{4,8},{8,12},{12,16},{16,20},{20,24},{24,28},{28,32},{32,36}... | collective-permute-start | bytes 3538952 | tf_op jit(solution)/shard_map/while/body/eval_jaxpr/ppermute | solution.py:10
  725.1 19.3 %collective-permute-start.1 = (f32[2,128,1152]{2,1,0:T(8,128)}, f32[2,128,1152]{2,1,0:T(8,128)}, u32[]{:S(2)}, u32[]{:S(2)}) collective-permute-start(f32[2,128,1152]{2,1,0:T(8,128)} %pad_maximum_fusion.5), channel_id=1, source_target_pairs={{0,4},{4,8},{8,12},{12,16},{16,20},{20,24},{24,28},{28,32},{32,36}... | collective-permute-start | bytes 3538952 | tf_op jit(solution)/shard_map/while/body/eval_jaxpr/ppermute | solution.py:10
  725.1 2.2 copy-start.2
  749.8 19.0 %collective-permute-start = (f32[2,128,1152]{2,1,0:T(8,128)S(1)}, f32[2,128,1152]{2,1,0:T(8,128)S(1)}, u32[]{:S(2)}, u32[]{:S(2)}) collective-permute-start(f32[2,128,1152]{2,1,0:T(8,128)S(1)} %pad_maximum_fusion.4), channel_id=1, source_target_pairs={{0,4},{4,8},{8,12},{12,16},{16,20},{20,24},{24,28},{28,32},{32,36}... | collective-permute-start | bytes 3538952 | tf_op jit(solution)/shard_map/while/body/eval_jaxpr/ppermute | solution.py:10
  773.9 19.3 %collective-permute-start.1 = (f32[2,128,1152]{2,1,0:T(8,128)}, f32[2,128,1152]{2,1,0:T(8,128)}, u32[]{:S(2)}, u32[]{:S(2)}) collective-permute-start(f32[2,128,1152]{2,1,0:T(8,128)} %pad_maximum_fusion.5), channel_id=1, source_target_pairs={{0,4},{4,8},{8,12},{12,16},{16,20},{20,24},{24,28},{28,32},{32,36}... | collective-permute-start | bytes 3538952 | tf_op jit(solution)/shard_map/while/body/eval_jaxpr/ppermute | solution.py:10
  773.9 2.2 copy-start.2
  798.6 19.0 %collective-permute-start = (f32[2,128,1152]{2,1,0:T(8,128)S(1)}, f32[2,128,1152]{2,1,0:T(8,128)S(1)}, u32[]{:S(2)}, u32[]{:S(2)}) collective-permute-start(f32[2,128,1152]{2,1,0:T(8,128)S(1)} %pad_maximum_fusion.4), channel_id=1, source_target_pairs={{0,4},{4,8},{8,12},{12,16},{16,20},{20,24},{24,28},{28,32},{32,36}... | collective-permute-start | bytes 3538952 | tf_op jit(solution)/shard_map/while/body/eval_jaxpr/ppermute | solution.py:10
  822.7 19.3 %collective-permute-start.1 = (f32[2,128,1152]{2,1,0:T(8,128)}, f32[2,128,1152]{2,1,0:T(8,128)}, u32[]{:S(2)}, u32[]{:S(2)}) collective-permute-start(f32[2,128,1152]{2,1,0:T(8,128)} %pad_maximum_fusion.5), channel_id=1, source_target_pairs={{0,4},{4,8},{8,12},{12,16},{16,20},{20,24},{24,28},{28,32},{32,36}... | collective-permute-start | bytes 3538952 | tf_op jit(solution)/shard_map/while/body/eval_jaxpr/ppermute | solution.py:10
  822.7 2.2 copy-start.2
  843.2 3.4 copy-start.6
  846.7 1.1 copy-start.4
  847.7 1.4 copy-start.7
  (27 other events, 16.9 us)
Sparse Core Ops, SparseCore 0:
  10.6 35.4 all-gather.3
  62.8 32.9 reduce-scatter.1
where the time goes:
time: 860 us; the launch traced here: 857 us
  waiting for transfers between devices  555 us (65%)
  matrix products  173 us (20%)
  local copies, waits for them, and re-layouts  56 us (7%)
  blocking collectives  27.2 us (3%)
  other arithmetic  26.9 us (3%)
  between operations  15.5 us (2%)
    ppermute x32, waiting for transfers between devices, passed_along(): return lax.ppermute(value, axis, pairs)  555 us
    dot_general x99, matrix products, product(): jnp.dot(left, right, precision=lax.Precision.HIGHEST, preferred_element_t...  173 us
    while x112, local copies, waits for them, and re-layouts  39.5 us
    another operation x32, other arithmetic, advance(): moved = passed_along(jnp.stack([state[0], state[1] + txt_part]), 'blk', 1)  19.3 us
  transfers between devices with their start and end apart: 34, of which 32 were waited for; matrix products, arithmetic and copies ran while one was open for 26% of the time, Pallas kernels for 0%

commit v1 on v0

v1 whole, which is shorter than its diff:
```python
import functools

import jax
import jax.numpy as jnp
from jax import lax
from jax.experimental import pallas as pl
from jax.experimental.pallas import tpu as pltpu
from jax.sharding import PartitionSpec as P

ROWS = 128
HALF = 64
PIECE = 32
D = 1152
COLS = ((0, 256), (256, 256), (512, 256), (768, 256), (1024, 128))
N_COPIES = 80
F32 = jnp.float32
BF16 = jnp.bfloat16


def rows_at(start, count):
    return pl.ds(start, count)


def split(values):
    high = values.astype(BF16)
    return high, (values - high.astype(F32)).astype(BF16)


def dot_nn(a, b):
    return lax.dot_general(a, b, (((1,), (0,)), ((), ())), preferred_element_type=F32)


def dot_nt(a, b):
    return lax.dot_general(a, b, (((1,), (1,)), ((), ())), preferred_element_type=F32)


def kernel(
    scale_ref, bias_ref, img_ref, txt_ref, pos_ref, cnt_ref, row_ref,
    gimg_ref, gtxt_ref,
    img, txt, img_hi, img_lo, txt_hi, txt_lo, sig, g_img, g_txt,
    y_txt, y_img, yt_hi, yt_lo, yi_hi, yi_lo,
    x_in, z_in, c_in, meta, mark_a, mark_b, norm_img, norm_txt, send_sem, recv_sem,
):
    blk, grp = lax.axis_index("blk"), lax.axis_index("grp")
    core = lax.rem(blk, 2)
    x = lax.rem(lax.div(blk, 2), 4)
    z = lax.div(blk, 8)

    def place(dz, dx, dg):
        zz, xx, gg = lax.rem(z + dz, 4), lax.rem(x + dx, 4), lax.rem(grp + dg, 4)
        return ((zz * 4 + xx) * 2 + core, gg)

    x_dev = (place(0, 1, 0), place(0, 3, 0))
    z_dev = (place(1, 0, 0), place(3, 0, 0))
    y_dev = (place(0, 0, 1), place(0, 0, 3))
    y_far = place(0, 0, 2)
    peer = ((z * 4 + x) * 2 + 1 - core, grp)
    partners = x_dev + z_dev + y_dev + (y_far, peer)

    barrier = pltpu.get_barrier_semaphore()
    for other in partners:
        pl.semaphore_signal(barrier, inc=1, device_id=other, device_id_type=pl.DeviceIdType.MESH)

    temper = scale_ref[0]
    offset = bias_ref[0]

    for source, unit, norm in ((img_ref, img, norm_img), (txt_ref, txt, norm_txt)):
        values = source[...]
        length = jnp.sqrt(jnp.sum(values * values, axis=1, keepdims=True) + 1e-06)
        norm[...] = length
        unit[0:ROWS, :] = values / length
    meta[0, 0:4, :] = pos_ref[...]
    meta[0, 4:5, :] = cnt_ref[...]
    meta[0, 5:6, :] = row_ref[...]
    meta[0, 6:8, :] = jnp.zeros((2, ROWS), jnp.int32)

    pl.semaphore_wait(barrier, len(partners))

    copies = {}

    def push(name, source, target, device):
        at = len(copies)
        copy = pltpu.make_async_remote_copy(
            src_ref=source, dst_ref=target, send_sem=send_sem.at[at], recv_sem=recv_sem.at[at],
            device_id=device, device_id_type=pl.DeviceIdType.MESH,
        )
        copy.start()
        copies[name] = copy

    def arrived(name):
        copies[name].wait_recv()

    rings = {"x": (img, 2 * ROWS, x_dev), "z": (txt, ROWS, z_dev)}

    def gather(axis, step, side, part):
        buffer, stride, devices = rings[axis]
        first = {1: side * HALF, 2: stride + side * HALF, 3: (1 - side) * HALF}[step]
        push(
            (axis, step, side, part),
            buffer.at[rows_at(first + part * PIECE, PIECE)],
            buffer.at[rows_at(stride * step + side * HALF + part * PIECE, PIECE)],
            devices[side],
        )

    y_rings = {"yt": (txt, y_txt), "yi": (img, y_img)}

    def gather_y(axis, step, side):
        own, others = y_rings[axis]
        half = side if step != 2 else 1 - side
        if step == 3:
            source = others.at[rows_at(side * ROWS + side * HALF, HALF)]
            target = others.at[rows_at(2 * ROWS + side * HALF, HALF)]
        else:
            source = own.at[rows_at(half * HALF, HALF)]
            target = others.at[rows_at(side * ROWS + half * HALF, HALF)]
        push((axis, step, side), source, target, y_dev[side])

    def across(step):
        first = 2 * ROWS * step
        push(("c", step), img.at[rows_at(first, ROWS)], img.at[rows_at(first + ROWS, ROWS)], peer)

    def split_rows(source, high, low, first, count):
        for at in range(first, first + count, HALF):
            high[at:at + HALF, :], low[at:at + HALF, :] = split(source[at:at + HALF, :])

    def sigmoids(row, rows, col, cols):
        def one(at, count):
            a_hi, a_lo = img_hi[rows_at(at, count), :], img_lo[rows_at(at, count), :]
            b_hi, b_lo = txt_hi[col:col + cols, :], txt_lo[col:col + cols, :]
            dots = dot_nt(a_hi, b_hi) + (dot_nt(a_hi, b_lo) + dot_nt(a_lo, b_hi))
            sig[rows_at(at, count), col:col + cols] = jax.nn.sigmoid(temper * dots + offset)

        if rows <= 256:
            one(row, rows)
        else:
            def turn(i, carry):
                one(pl.multiple_of(row + i * 256, 256), 256)
                return carry

            lax.fori_loop(0, rows // 256, turn, 0)

    def times(left, high, low, store):
        l_hi, l_lo = split(left)
        for at, count in COLS:
            cs = slice(at, at + count)
            store(cs, dot_nn(l_hi, high[:, cs]) + (dot_nn(l_hi, low[:, cs]) + dot_nn(l_lo, high[:, cs])))

    def image_grads(first):
        def store(cs, value):
            g_img[first:first + ROWS, cs] = value

        times(sig[first:first + ROWS, :], txt_hi, txt_lo, store)

    def text_grads(first):
        def store(cs, value):
            g_txt[first:first + ROWS, cs] = value

        times(sig[:, first:first + ROWS].T, img_hi, img_lo, store)

    for slot, device in ((1, y_dev[0]), (2, y_dev[1]), (3, y_far)):
        push(("m", slot), meta.at[0], meta.at[slot], device)
    for part in (0, 1):
        for axis in ("x", "z"):
            for side in (0, 1):
                gather(axis, 1, side, part)
    across(0)
    for step in (1, 2):
        for side in (0, 1):
            gather_y("yt", step, side)

    split_rows(img, img_hi, img_lo, 0, ROWS)
    split_rows(txt, txt_hi, txt_lo, 0, ROWS)
    arrived(("c", 0))
    split_rows(img, img_hi, img_lo, ROWS, ROWS)
    sigmoids(0, 256, 0, ROWS)

    for slot in (1, 2, 3):
        arrived(("m", slot))
    group_base = blk * (4 * ROWS)
    places = [lax.rem(grp + shift, 4) * ROWS + group_base for shift in (0, 3, 1, 2)]
    tall = lax.broadcasted_iota(jnp.int32, (ROWS, ROWS), 0)

    def named(slot):
        tiles = []
        for ids in range(4):
            hit = None
            for k in range(4):
                listed = jnp.where(meta[slot, 4:5, :] > k, meta[slot, k:k + 1, :], -1)
                same = listed == tall + places[ids]
                hit = same if hit is None else hit | same
            tiles.append(jnp.where(hit, 1.0, 0.0).astype(BF16))
        return jnp.concatenate(tiles, axis=0)

    def held(slot):
        tiles = [
            jnp.where(meta[ids, 5:6, :] == tall + places[slot], 1.0, 0.0).astype(BF16)
            for ids in range(4)
        ]
        return jnp.concatenate(tiles, axis=1)

    for part in (0, 1):
        for axis in ("x", "z"):
            for side in (0, 1):
                arrived((axis, 1, side, part))
                gather(axis, 2, side, part)
    across(1)
    for part in (0, 1):
        for axis in ("x", "z"):
            for side in (0, 1):
                gather(axis, 3, side, part)
    for side in (0, 1):
        arrived(("yt", 1, side))
        gather_y("yt", 3, side)
    for step in (1, 2):
        for side in (0, 1):
            gather_y("yi", step, side)

    split_rows(txt, txt_hi, txt_lo, ROWS, ROWS)
    split_rows(img, img_hi, img_lo, 256, ROWS)
    arrived(("c", 1))
    split_rows(img, img_hi, img_lo, 256 + ROWS, ROWS)
    sigmoids(256, 256, 0, 256)
    sigmoids(0, 256, ROWS, ROWS)

    own_ids, own_held = named(0), held(0)
    mark_a[:, 0:ROWS] = dot_nn(own_held, own_ids)
    for slot in (1, 2, 3):
        mark_a[:, slot * ROWS:(slot + 1) * ROWS] = dot_nn(own_held, named(slot))
        mark_b[(slot - 1) * ROWS:slot * ROWS, :] = dot_nn(held(slot), own_ids)

    for part in (0, 1):
        for axis in ("x", "z"):
            for side in (0, 1):
                arrived((axis, 2, side, part))
    across(2)
    split_rows(txt, txt_hi, txt_lo, 2 * ROWS, ROWS)
    split_rows(img, img_hi, img_lo, 512, ROWS)
    arrived(("c", 2))
    split_rows(img, img_hi, img_lo, 512 + ROWS, ROWS)
    sigmoids(512, 256, 0, 3 * ROWS)
    sigmoids(0, 512, 2 * ROWS, ROWS)

    for part in (0, 1):
        for side in (0, 1):
            arrived(("x", 3, side, part))
    across(3)
    for part in (0, 1):
        for side in (0, 1):
            arrived(("z", 3, side, part))
    split_rows(txt, txt_hi, txt_lo, 3 * ROWS, ROWS)
    sigmoids(512, 256, 3 * ROWS, ROWS)

    def share(step):
        first = 2 * ROWS * step
        push(("r", step), g_img.at[rows_at(first + ROWS, ROWS)], c_in.at[step], peer)

    def joined(step):
        first = 2 * ROWS * step
        arrived(("r", step))
        g_img[first:first + ROWS, :] += c_in[step]

    scatters = {"x": (g_img, 2 * ROWS, x_dev, x_in), "z": (g_txt, ROWS, z_dev, z_in)}

    def scatter(axis, turn):
        buffer, stride, devices, inbox = scatters[axis]
        for side in (0, 1):
            first = (2 * stride + side * HALF, stride + (1 - side) * HALF, 3 * stride + (1 - side) * HALF)[turn]
            if turn == 2:
                arrived((axis, "s", 0, side))
                buffer[first:first + HALF, :] += inbox[side, 0]
            push((axis, "s", turn, side), buffer.at[rows_at(first, HALF)], inbox.at[side, turn], devices[side])

    image_grads(512 + ROWS)
    share(2)
    image_grads(512)
    split_rows(img, img_hi, img_lo, 768, ROWS)
    arrived(("c", 3))
    split_rows(img, img_hi, img_lo, 768 + ROWS, ROWS)
    sigmoids(768, 256, 2 * ROWS, ROWS)
    joined(2)
    scatter("x", 0)
    text_grads(2 * ROWS)
    scatter("z", 0)

    sigmoids(0, 512, 3 * ROWS, ROWS)
    image_grads(256 + ROWS)
    share(1)
    image_grads(256)
    sigmoids(768, 256, 0, 2 * ROWS)
    joined(1)
    scatter("x", 1)
    text_grads(ROWS)
    scatter("z", 1)

    sigmoids(768, 256, 3 * ROWS, ROWS)
    image_grads(768 + ROWS)
    share(3)
    image_grads(768)
    joined(3)
    scatter("x", 2)
    text_grads(3 * ROWS)
    scatter("z", 2)

    for side in (0, 1):
        arrived(("yi", 1, side))
        gather_y("yi", 3, side)

    image_grads(ROWS)
    share(0)
    sig[0:ROWS, 0:ROWS] -= mark_a[:, 0:ROWS]
    image_grads(0)
    text_grads(0)

    for side in (0, 1):
        arrived(("yt", 2, side))
        arrived(("yt", 3, side))
    split_rows(y_txt, yt_hi, yt_lo, 0, 3 * ROWS)
    own = rows_at(0, ROWS)
    dots = dot_nt(img_hi[own, :], yt_hi[...]) + (dot_nt(img_hi[own, :], yt_lo[...]) + dot_nt(img_lo[own, :], yt_hi[...]))
    coef = mark_a[:, ROWS:4 * ROWS] * (jax.nn.sigmoid(temper * dots + offset) - 1.0)

    def add_img(cs, value):
        g_img[0:ROWS, cs] += value

    times(coef, yt_hi, yt_lo, add_img)
    joined(0)

    for side in (0, 1):
        arrived(("yi", 2, side))
        arrived(("yi", 3, side))
    split_rows(y_img, yi_hi, yi_lo, 0, 3 * ROWS)
    dots = dot_nt(yi_hi[...], txt_hi[own, :]) + (dot_nt(yi_hi[...], txt_lo[own, :]) + dot_nt(yi_lo[...], txt_hi[own, :]))
    coef = mark_b[...] * (jax.nn.sigmoid(temper * dots + offset) - 1.0)

    def add_txt(cs, value):
        g_txt[0:ROWS, cs] += value

    times(coef.T, yi_hi, yi_lo, add_txt)

    for axis, sums, inbox, unit, norm, out in (
        ("x", g_img, x_in, img, norm_img, gimg_ref),
        ("z", g_txt, z_in, txt, norm_txt, gtxt_ref),
    ):
        for turn in (1, 2):
            for side in (0, 1):
                arrived((axis, "s", turn, side))
        for half in (0, 1):
            at = slice(half * HALF, (half + 1) * HALF)
            grad = temper * (sums[at, :] + inbox[1 - half, 1] + inbox[half, 2])
            units = unit[at, :]
            along = jnp.sum(units * grad, axis=1, keepdims=True)
            out[at, :] = (grad - units * along) / norm[at, :]

    for copy in copies.values():
        copy.wait_send()


def body(image_emb, text_emb, logit_scale, logit_bias, pos_image, pos_count, image_row):
    smem = pl.BlockSpec(memory_space=pltpu.SMEM)
    vmem = pl.BlockSpec(memory_space=pltpu.VMEM)
    rows = jax.ShapeDtypeStruct((ROWS, D), F32)
    return pl.pallas_call(
        kernel,
        out_shape=(rows, rows),
        in_specs=[smem, smem, vmem, vmem, vmem, vmem, vmem],
        out_specs=(vmem, vmem),
        scratch_shapes=[
            pltpu.VMEM((8 * ROWS, D), F32),
            pltpu.VMEM((4 * ROWS, D), F32),
            pltpu.VMEM((8 * ROWS, D), BF16),
            pltpu.VMEM((8 * ROWS, D), BF16),
            pltpu.VMEM((4 * ROWS, D), BF16),
            pltpu.VMEM((4 * ROWS, D), BF16),
            pltpu.VMEM((8 * ROWS, 4 * ROWS), F32),
            pltpu.VMEM((8 * ROWS, D), F32),
            pltpu.VMEM((4 * ROWS, D), F32),
            pltpu.VMEM((3 * ROWS, D), F32),
            pltpu.VMEM((3 * ROWS, D), F32),
            pltpu.VMEM((3 * ROWS, D), BF16),
            pltpu.VMEM((3 * ROWS, D), BF16),
            pltpu.VMEM((3 * ROWS, D), BF16),
            pltpu.VMEM((3 * ROWS, D), BF16),
            pltpu.VMEM((2, 3, HALF, D), F32),
            pltpu.VMEM((2, 3, HALF, D), F32),
            pltpu.VMEM((4, ROWS, D), F32),
            pltpu.VMEM((4, 8, ROWS), jnp.int32),
            pltpu.VMEM((ROWS, 4 * ROWS), F32),
            pltpu.VMEM((3 * ROWS, ROWS), F32),
            pltpu.VMEM((ROWS, 1), F32),
            pltpu.VMEM((ROWS, 1), F32),
            pltpu.SemaphoreType.DMA((N_COPIES,)),
            pltpu.SemaphoreType.DMA((N_COPIES,)),
        ],
        compiler_params=pltpu.CompilerParams(
            collective_id=0, has_side_effects=True, vmem_limit_bytes=56 * 2**20
        ),
        name="align_step",
    )(
        logit_scale, logit_bias, image_emb, text_emb,
        pos_image.T, pos_count.reshape(1, ROWS), image_row.reshape(1, ROWS),
    )


def solution(mesh):
    return jax.shard_map(
        body,
        mesh=mesh,
        in_specs=(
            P(("blk", "grp"), None),
            P(("blk", "grp"), None),
            P(),
            P(),
            P(("blk", "grp"), None),
            P(("blk", "grp")),
            P(("blk", "grp")),
        ),
        out_specs=(P(("blk", "grp"), None), P(("blk", "grp"), None)),
        check_vma=False,
    )
```

time: 860 us -> 63.9 us (0.07)
  waiting for transfers between devices: 555 us -> 0 us
  matrix products: 173 us -> 0 us
  Pallas kernels: 0 us -> 58.2 us
  local copies, waits for them, and re-layouts: 56 us -> 2.8 us
  blocking collectives: 27.2 us -> 0 us
  other arithmetic: 26.9 us -> 0 us
  between operations: 15.5 us -> 1.94 us
    ppermute x32 -> x0, waiting for transfers between devices: 555 us -> none  [passed_along(): return lax.ppermute(value, axis, pairs)]
    dot_general x99 -> x0, matrix products: 173 us -> none  [product(): jnp.dot(left, right, precision=lax.Precision.HIGHEST, preferred_element_t...]
    pallas_call x0 -> x1, Pallas kernels: none -> 58.2 us  [body(): pl.pallas_call(kernel, out_shape=(rows, rows), in_specs=[smem, smem, vmem...]
    while x112 -> x0, local copies, waits for them, and re-layouts: 39.5 us -> none
    all_gather x3 -> x0, blocking collectives: 27.2 us -> none  [the longest x1 11.3 us: body(): lax.all_gather(pos_image, 'grp', axis=0, tiled=True)]
    another operation x33 -> x0, other arithmetic: 19.4 us -> none  [the longest x32 19.3 us: advance(): moved = passed_along(jnp.stack([state[0], state[1] + txt_part]), 'blk', 1)]
    gather x3 -> x0, local copies, waits for them, and re-layouts: 13.6 us -> none  [body(): target = jnp.take(id_rows, lists - group_base, axis=0)]
  transfers between devices with their start and end apart: 34 -> 0, of which waited for: 32 -> 0; matrix products, arithmetic and copies ran while one was open for 26% -> 0% of each run, Pallas kernels for 0% -> 0%
where the time goes in v1:
time: 63.9 us; the launch traced here: 63 us
  Pallas kernels  58.2 us (91%)
  local copies, waits for them, and re-layouts  2.8 us (4%)
  between operations  1.94 us (3%)
    pallas_call x1, Pallas kernels, body(): pl.pallas_call(kernel, out_shape=(rows, rows), in_specs=[smem, smem, vmem...  58.2 us
    unnamed x4, local copies, waits for them, and re-layouts  2.8 us

profile of v1, /device:TPU:0, one launch (start us, length us, event | category | flops | bytes accessed | tf_op | source)
XLA Modules:
  0.0 63.0 jit_solution(7274510268139686844)
XLA Ops:
  1.9 58.2 %align_step.1 = (f32[128,1152]{1,0:T(8,128)}, f32[128,1152]{1,0:T(8,128)}) custom-call(f32[1]{0:T(128)S(6)} %copy.11.scale_ref, f32[1]{0:T(128)S(6)} %copy.12.bias_ref, f32[128,1152]{1,0:T(8,128)} %img_ref.1, f32[128,1152]{1,0:T(8,128)} %txt_ref.1, s32[4,128]{1,0:T(4,128)} %bitcast.3, s32[1,128]{1,0:T(1,128)} %bitcast.4, s32[1,128]{1,0:T(1,128)} %bitcast.5), custom_call_target="tpu_custom_call" | custom-call | tf_op jit(solution)/shard_map/align_step/pallas_call | solution.py:362
  60.1 0.0 copy-start
  60.2 2.0 %copy.13 = f32[128,1152]{1,0:T(8,128)} copy(f32[128,1152]{1,0:T(8,128)} %get-tuple-element.4) | data formatting | bytes 1179648
  62.1 0.0 copy-done
  62.1 0.8 %copy.14 = f32[128,1152]{1,0:T(8,128)} copy(f32[128,1152]{1,0:T(8,128)S(1)} %copy-done) | data formatting | bytes 1179648
Async XLA Ops:
  60.1 2.0 %copy-start = (f32[128,1152]{1,0:T(8,128)S(1)}, f32[128,1152]{1,0:T(8,128)}, u32[]{:S(2)}) copy-start(f32[128,1152]{1,0:T(8,128)} %get-tuple-element.5) | copy-start | bytes 1769476

commit v2 on v1

--- a/solution.py
+++ b/solution.py
@@ -35,8 +35,9 @@
 
 
 def kernel(
-    scale_ref, bias_ref, img_ref, txt_ref, pos_ref, cnt_ref, row_ref,
+    scale_ref, bias_ref, img_hbm, txt_hbm, pos_hbm, cnt_hbm, row_hbm,
     gimg_ref, gtxt_ref,
+    img_ref, txt_ref, pos_ref, cnt_ref, row_ref, load_sem,
     img, txt, img_hi, img_lo, txt_hi, txt_lo, sig, g_img, g_txt,
     y_txt, y_img, yt_hi, yt_lo, yi_hi, yi_lo,
     x_in, z_in, c_in, meta, mark_a, mark_b, norm_img, norm_txt, send_sem, recv_sem,
@@ -60,6 +61,18 @@
     barrier = pltpu.get_barrier_semaphore()
     for other in partners:
         pl.semaphore_signal(barrier, inc=1, device_id=other, device_id_type=pl.DeviceIdType.MESH)
+
+    loads = [
+        pltpu.make_async_copy(source, target, load_sem.at[at])
+        for at, (source, target) in enumerate((
+            (img_hbm, img_ref), (txt_hbm, txt_ref), (pos_hbm, pos_ref), (cnt_hbm, cnt_ref),
+            (row_hbm, row_ref),
+        ))
+    ]
+    for load in loads:
+        load.start()
+    for load in loads:
+        load.wait()
 
     temper = scale_ref[0]
     offset = bias_ref[0]
@@ -145,17 +158,17 @@
             cs = slice(at, at + count)
             store(cs, dot_nn(l_hi, high[:, cs]) + (dot_nn(l_hi, low[:, cs]) + dot_nn(l_lo, high[:, cs])))
 
-    def image_grads(first):
+    def image_grads(first, col=0, cols=4 * ROWS, add=False):
         def store(cs, value):
-            g_img[first:first + ROWS, cs] = value
-
-        times(sig[first:first + ROWS, :], txt_hi, txt_lo, store)
-
-    def text_grads(first):
+            g_img[first:first + ROWS, cs] = g_img[first:first + ROWS, cs] + value if add else value
+
+        times(sig[first:first + ROWS, col:col + cols], txt_hi.at[col:col + cols], txt_lo.at[col:col + cols], store)
+
+    def text_grads(first, row=0, rows=8 * ROWS, add=False):
         def store(cs, value):
-            g_txt[first:first + ROWS, cs] = value
-
-        times(sig[:, first:first + ROWS].T, img_hi, img_lo, store)
+            g_txt[first:first + ROWS, cs] = g_txt[first:first + ROWS, cs] + value if add else value
+
+        times(sig[row:row + rows, first:first + ROWS].T, img_hi.at[row:row + rows], img_lo.at[row:row + rows], store)
 
     for slot, device in ((1, y_dev[0]), (2, y_dev[1]), (3, y_far)):
         push(("m", slot), meta.at[0], meta.at[slot], device)
@@ -198,11 +211,21 @@
         ]
         return jnp.concatenate(tiles, axis=1)
 
-    for part in (0, 1):
-        for axis in ("x", "z"):
-            for side in (0, 1):
-                arrived((axis, 1, side, part))
-                gather(axis, 2, side, part)
+    for axis in ("x", "z"):
+        for side in (0, 1):
+            arrived((axis, 1, side, 0))
+            gather(axis, 2, side, 0)
+
+    own_ids, own_held = named(0), held(0)
+    mark_a[:, 0:ROWS] = dot_nn(own_held, own_ids)
+    for slot in (1, 2, 3):
+        mark_a[:, slot * ROWS:(slot + 1) * ROWS] = dot_nn(own_held, named(slot))
+        mark_b[(slot - 1) * ROWS:slot * ROWS, :] = dot_nn(held(slot), own_ids)
+
+    for axis in ("x", "z"):
+        for side in (0, 1):
+            arrived((axis, 1, side, 1))
+            gather(axis, 2, side, 1)
     across(1)
     for part in (0, 1):
         for axis in ("x", "z"):
@@ -217,16 +240,10 @@
 
     split_rows(txt, txt_hi, txt_lo, ROWS, ROWS)
     split_rows(img, img_hi, img_lo, 256, ROWS)
+    sigmoids(0, 256, ROWS, ROWS)
     arrived(("c", 1))
     split_rows(img, img_hi, img_lo, 256 + ROWS, ROWS)
     sigmoids(256, 256, 0, 256)
-    sigmoids(0, 256, ROWS, ROWS)
-
-    own_ids, own_held = named(0), held(0)
-    mark_a[:, 0:ROWS] = dot_nn(own_held, own_ids)
-    for slot in (1, 2, 3):
-        mark_a[:, slot * ROWS:(slot + 1) * ROWS] = dot_nn(own_held, named(slot))
-        mark_b[(slot - 1) * ROWS:slot * ROWS, :] = dot_nn(held(slot), own_ids)
 
     for part in (0, 1):
         for axis in ("x", "z"):
@@ -235,10 +252,13 @@
     across(2)
     split_rows(txt, txt_hi, txt_lo, 2 * ROWS, ROWS)
     split_rows(img, img_hi, img_lo, 512, ROWS)
+    sigmoids(0, 512, 2 * ROWS, ROWS)
     arrived(("c", 2))
     split_rows(img, img_hi, img_lo, 512 + ROWS, ROWS)
     sigmoids(512, 256, 0, 3 * ROWS)
-    sigmoids(0, 512, 2 * ROWS, ROWS)
+    text_grads(2 * ROWS, 0, 768)
+    image_grads(512 + ROWS, 0, 3 * ROWS)
+    image_grads(512, 0, 3 * ROWS)
 
     for part in (0, 1):
         for side in (0, 1):
@@ -247,8 +267,6 @@
     for part in (0, 1):
         for side in (0, 1):
             arrived(("z", 3, side, part))
-    split_rows(txt, txt_hi, txt_lo, 3 * ROWS, ROWS)
-    sigmoids(512, 256, 3 * ROWS, ROWS)
 
     def share(step):
         first = 2 * ROWS * step
@@ -270,17 +288,19 @@
                 buffer[first:first + HALF, :] += inbox[side, 0]
             push((axis, "s", turn, side), buffer.at[rows_at(first, HALF)], inbox.at[side, turn], devices[side])
 
-    image_grads(512 + ROWS)
+    split_rows(txt, txt_hi, txt_lo, 3 * ROWS, ROWS)
+    sigmoids(512, 256, 3 * ROWS, ROWS)
+    image_grads(512 + ROWS, 3 * ROWS, ROWS, True)
     share(2)
-    image_grads(512)
+    image_grads(512, 3 * ROWS, ROWS, True)
     split_rows(img, img_hi, img_lo, 768, ROWS)
     arrived(("c", 3))
     split_rows(img, img_hi, img_lo, 768 + ROWS, ROWS)
     sigmoids(768, 256, 2 * ROWS, ROWS)
+    text_grads(2 * ROWS, 768, 256, True)
+    scatter("z", 0)
     joined(2)
     scatter("x", 0)
-    text_grads(2 * ROWS)
-    scatter("z", 0)
 
     sigmoids(0, 512, 3 * ROWS, ROWS)
     image_grads(256 + ROWS)
@@ -292,18 +312,18 @@
     text_grads(ROWS)
     scatter("z", 1)
 
+    for side in (0, 1):
+        arrived(("yi", 1, side))
+        gather_y("yi", 3, side)
+
     sigmoids(768, 256, 3 * ROWS, ROWS)
     image_grads(768 + ROWS)
     share(3)
     image_grads(768)
+    text_grads(3 * ROWS)
     joined(3)
     scatter("x", 2)
-    text_grads(3 * ROWS)
     scatter("z", 2)
-
-    for side in (0, 1):
-        arrived(("yi", 1, side))
-        gather_y("yi", 3, side)
 
     image_grads(ROWS)
     share(0)
@@ -337,16 +357,21 @@
 
     times(coef.T, yi_hi, yi_lo, add_txt)
 
-    for axis, sums, inbox, unit, norm, out in (
+    ends = (
         ("x", g_img, x_in, img, norm_img, gimg_ref),
         ("z", g_txt, z_in, txt, norm_txt, gtxt_ref),
-    ):
-        for turn in (1, 2):
-            for side in (0, 1):
-                arrived((axis, "s", turn, side))
+    )
+    for axis, sums, inbox, unit, norm, out in ends:
+        for side in (0, 1):
+            at = slice((1 - side) * HALF, (2 - side) * HALF)
+            arrived((axis, "s", 1, side))
+            sums[at, :] += inbox[side, 1]
+    for axis, sums, inbox, unit, norm, out in ends:
+        for side in (0, 1):
+            arrived((axis, "s", 2, side))
         for half in (0, 1):
             at = slice(half * HALF, (half + 1) * HALF)
-            grad = temper * (sums[at, :] + inbox[1 - half, 1] + inbox[half, 2])
+            grad = temper * (sums[at, :] + inbox[half, 2])
             units = unit[at, :]
             along = jnp.sum(units * grad, axis=1, keepdims=True)
             out[at, :] = (grad - units * along) / norm[at, :]
@@ -355,16 +380,33 @@
         copy.wait_send()
 
 
+def hand_on(gimg_in, gtxt_in, gimg_out, gtxt_out, sems):
+    copies = [
+        pltpu.make_async_copy(gimg_in, gimg_out, sems.at[0]),
+        pltpu.make_async_copy(gtxt_in, gtxt_out, sems.at[1]),
+    ]
+    for copy in copies:
+        copy.start()
+    for copy in copies:
+        copy.wait()
+
+
 def body(image_emb, text_emb, logit_scale, logit_bias, pos_image, pos_count, image_row):
-    smem = pl.BlockSpec(memory_space=pltpu.SMEM)
+    anywhere = pl.BlockSpec(memory_space=pl.ANY)
     vmem = pl.BlockSpec(memory_space=pltpu.VMEM)
     rows = jax.ShapeDtypeStruct((ROWS, D), F32)
-    return pl.pallas_call(
+    grads = pl.pallas_call(
         kernel,
-        out_shape=(rows, rows),
-        in_specs=[smem, smem, vmem, vmem, vmem, vmem, vmem],
+        out_shape=(pltpu.VMEM((ROWS, D), F32), pltpu.VMEM((ROWS, D), F32)),
+        in_specs=[pl.BlockSpec(memory_space=pltpu.SMEM)] * 2 + [pl.BlockSpec(memory_space=pltpu.HBM)] * 5,
         out_specs=(vmem, vmem),
         scratch_shapes=[
+            pltpu.VMEM((ROWS, D), F32),
+            pltpu.VMEM((ROWS, D), F32),
+            pltpu.VMEM((4, ROWS), jnp.int32),
+            pltpu.VMEM((1, ROWS), jnp.int32),
+            pltpu.VMEM((1, ROWS), jnp.int32),
+            pltpu.SemaphoreType.DMA((5,)),
             pltpu.VMEM((8 * ROWS, D), F32),
             pltpu.VMEM((4 * ROWS, D), F32),
             pltpu.VMEM((8 * ROWS, D), BF16),
@@ -392,13 +434,28 @@
             pltpu.SemaphoreType.DMA((N_COPIES,)),
         ],
         compiler_params=pltpu.CompilerParams(
-            collective_id=0, has_side_effects=True, vmem_limit_bytes=56 * 2**20
+            collective_id=0, has_side_effects=True, vmem_limit_bytes=42 * 2**20
         ),
         name="align_step",
     )(
-        logit_scale, logit_bias, image_emb, text_emb,
-        pos_image.T, pos_count.reshape(1, ROWS), image_row.reshape(1, ROWS),
+        logit_scale,
+        logit_bias,
+        *(
+            pltpu.with_memory_space_constraint(operand, pltpu.HBM)
+            for operand in (
+                image_emb, text_emb, pos_image.T, pos_count.reshape(1, ROWS), image_row.reshape(1, ROWS),
+            )
+        ),
     )
+    grads = [pltpu.with_memory_space_constraint(grad, pltpu.VMEM) for grad in grads]
+    return pl.pallas_call(
+        hand_on,
+        out_shape=(rows, rows),
+        in_specs=[vmem, vmem],
+        out_specs=(anywhere, anywhere),
+        scratch_shapes=[pltpu.SemaphoreType.DMA((2,))],
+        name="hand_on",
+    )(*grads)
 
 
 def solution(mesh):

time: 63.9 us -> 58.5 us (0.915)
  local copies, waits for them, and re-layouts: 2.8 us -> 0 us
  Pallas kernels: 58.2 us -> 55.6 us
    unnamed x4 -> x0, local copies, waits for them, and re-layouts: 2.8 us -> none
    pallas_call x1 -> x2, Pallas kernels: 58.2 us -> 55.6 us  [the longest x1 54.6 us: body(): pl.pallas_call(kernel, out_shape=(pltpu.VMEM((ROWS, D), F32), pltpu.VMEM(...]
where the time goes in v2:
time: 58.5 us; the launch traced here: 57.7 us
  Pallas kernels  55.6 us (95%)
  between operations  2.09 us (4%)
    pallas_call x1, Pallas kernels, body(): pl.pallas_call(kernel, out_shape=(pltpu.VMEM((ROWS, D), F32), pltpu.VMEM(...  54.6 us

profile of v2, /device:TPU:0, one launch (start us, length us, event | category | flops | bytes accessed | tf_op | source)
XLA Modules:
  0.0 57.7 jit_solution(1402750581504683375)
XLA Ops:
  1.9 54.6 %align_step.1 = (f32[128,1152]{1,0:T(8,128)S(1)}, f32[128,1152]{1,0:T(8,128)S(1)}) custom-call(f32[1]{0:T(128)S(6)} %copy.9.scale_ref, f32[1]{0:T(128)S(6)} %copy.10.bias_ref, f32[128,1152]{1,0:T(8,128)} %img_hbm.1, f32[128,1152]{1,0:T(8,128)} %txt_hbm.1, s32[4,128]{1,0:T(4,128)} %bitcast.3, s32[1,128]{1,0:T(1,128)} %bitcast.4, s32[1,128]{1,0:T(1,128)} %bitcast.5), custom_call_target="tpu_custom_call" | custom-call | tf_op jit(solution)/shard_map/align_step/pallas_call | solution.py:398
  56.5 1.0 %hand_on.1 = (f32[128,1152]{1,0:T(8,128)}, f32[128,1152]{1,0:T(8,128)}) custom-call(f32[128,1152]{1,0:T(8,128)S(1)} %get-tuple-element.4.gimg_in, f32[128,1152]{1,0:T(8,128)S(1)} %get-tuple-element.5.gtxt_in), custom_call_target="tpu_custom_call" | custom-call | tf_op jit(solution)/shard_map/hand_on/pallas_call | solution.py:451

commit v3 on v2

--- a/solution.py
+++ b/solution.py
@@ -12,7 +12,9 @@
 PIECE = 32
 D = 1152
 COLS = ((0, 256), (256, 256), (512, 256), (768, 256), (1024, 128))
-N_COPIES = 80
+N_SEND = 5
+N_RECV = 33
+CORE, GATHER, ALONG_Y, SCATTER, LISTS = range(N_SEND)
 F32 = jnp.float32
 BF16 = jnp.bfloat16
 
@@ -40,7 +42,7 @@
     img_ref, txt_ref, pos_ref, cnt_ref, row_ref, load_sem,
     img, txt, img_hi, img_lo, txt_hi, txt_lo, sig, g_img, g_txt,
     y_txt, y_img, yt_hi, yt_lo, yi_hi, yi_lo,
-    x_in, z_in, c_in, meta, mark_a, mark_b, norm_img, norm_txt, send_sem, recv_sem,
+    txt_both, x_in, z_in, c_in, meta, mark_a, mark_b, norm_img, norm_txt, send_sem, recv_sem,
 ):
     blk, grp = lax.axis_index("blk"), lax.axis_index("grp")
     core = lax.rem(blk, 2)
@@ -62,58 +64,69 @@
     for other in partners:
         pl.semaphore_signal(barrier, inc=1, device_id=other, device_id_type=pl.DeviceIdType.MESH)
 
-    loads = [
-        pltpu.make_async_copy(source, target, load_sem.at[at])
-        for at, (source, target) in enumerate((
-            (img_hbm, img_ref), (txt_hbm, txt_ref), (pos_hbm, pos_ref), (cnt_hbm, cnt_ref),
-            (row_hbm, row_ref),
-        ))
-    ]
-    for load in loads:
-        load.start()
-    for load in loads:
-        load.wait()
-
     temper = scale_ref[0]
     offset = bias_ref[0]
-
-    for source, unit, norm in ((img_ref, img, norm_img), (txt_ref, txt, norm_txt)):
-        values = source[...]
-        length = jnp.sqrt(jnp.sum(values * values, axis=1, keepdims=True) + 1e-06)
-        norm[...] = length
-        unit[0:ROWS, :] = values / length
-    meta[0, 0:4, :] = pos_ref[...]
-    meta[0, 4:5, :] = cnt_ref[...]
-    meta[0, 5:6, :] = row_ref[...]
-    meta[0, 6:8, :] = jnp.zeros((2, ROWS), jnp.int32)
-
+    sources = ((img_hbm, img_ref, img, norm_img), (txt_hbm, txt_ref, txt, norm_txt))
+    for part in (0, 1):
+        for hbm, ref, _, _ in sources:
+            for half in (0, 1):
+                at = rows_at(half * HALF + part * PIECE, PIECE)
+                pltpu.make_async_copy(hbm.at[at], ref.at[at], load_sem.at[part]).start()
+    small = [
+        pltpu.make_async_copy(source, target, load_sem.at[2 + at])
+        for at, (source, target) in enumerate(((pos_hbm, pos_ref), (cnt_hbm, cnt_ref), (row_hbm, row_ref)))
+    ]
+    for load in small:
+        load.start()
+
+    def normalize(part):
+        pltpu.make_async_copy(img_hbm, img_ref, load_sem.at[part]).wait()
+        for _, ref, unit, norm in sources:
+            for half in (0, 1):
+                at = rows_at(half * HALF + part * PIECE, PIECE)
+                values = ref[at, :]
+                length = jnp.sqrt(jnp.sum(values * values, axis=1, keepdims=True) + 1e-06)
+                norm[at, :] = length
+                unit[at, :] = values / length
+
+    normalize(0)
     pl.semaphore_wait(barrier, len(partners))
 
-    copies = {}
-
-    def push(name, source, target, device):
-        at = len(copies)
-        copy = pltpu.make_async_remote_copy(
-            src_ref=source, dst_ref=target, send_sem=send_sem.at[at], recv_sem=recv_sem.at[at],
+    groups = {}
+
+    def push(group, source, target, device, send):
+        at = groups.setdefault(group, len(groups))
+        pltpu.make_async_remote_copy(
+            src_ref=source, dst_ref=target, send_sem=send_sem.at[send], recv_sem=recv_sem.at[at],
             device_id=device, device_id_type=pl.DeviceIdType.MESH,
-        )
-        copy.start()
-        copies[name] = copy
-
-    def arrived(name):
-        copies[name].wait_recv()
+        ).start()
+
+    def done(sem, region):
+        pltpu.make_async_copy(region, region, sem).wait()
+
+    def arrived(group, region):
+        done(recv_sem.at[groups[group]], region)
 
     rings = {"x": (img, 2 * ROWS, x_dev), "z": (txt, ROWS, z_dev)}
+
+    def piece(axis, step, side, part):
+        buffer, stride, _ = rings[axis]
+        return buffer.at[rows_at(stride * step + side * HALF + part * PIECE, PIECE)]
 
     def gather(axis, step, side, part):
         buffer, stride, devices = rings[axis]
         first = {1: side * HALF, 2: stride + side * HALF, 3: (1 - side) * HALF}[step]
         push(
-            (axis, step, side, part),
+            (axis, 1, side, part) if step == 1 else (axis, step),
             buffer.at[rows_at(first + part * PIECE, PIECE)],
-            buffer.at[rows_at(stride * step + side * HALF + part * PIECE, PIECE)],
+            piece(axis, step, side, part),
             devices[side],
+            GATHER,
         )
+
+    def gathered(axis, step):
+        buffer, stride, _ = rings[axis]
+        arrived((axis, step), buffer.at[rows_at(stride * step, ROWS)])
 
     y_rings = {"yt": (txt, y_txt), "yi": (img, y_img)}
 
@@ -126,22 +139,50 @@
         else:
             source = own.at[rows_at(half * HALF, HALF)]
             target = others.at[rows_at(side * ROWS + half * HALF, HALF)]
-        push((axis, step, side), source, target, y_dev[side])
+        push((axis, 1, side) if step == 1 else (axis, 2), source, target, y_dev[side], ALONG_Y)
+
+    def forward_y(axis):
+        others = y_rings[axis][1]
+        for side in (0, 1):
+            arrived((axis, 1, side), others.at[rows_at(side * ROWS + side * HALF, HALF)])
+            gather_y(axis, 3, side)
 
     def across(step):
         first = 2 * ROWS * step
-        push(("c", step), img.at[rows_at(first, ROWS)], img.at[rows_at(first + ROWS, ROWS)], peer)
+        push(("c", step), img.at[rows_at(first, ROWS)], img.at[rows_at(first + ROWS, ROWS)], peer, CORE)
+
+    def crossed(step):
+        arrived(("c", step), img.at[rows_at(2 * ROWS * step + ROWS, ROWS)])
 
     def split_rows(source, high, low, first, count):
         for at in range(first, first + count, HALF):
             high[at:at + HALF, :], low[at:at + HALF, :] = split(source[at:at + HALF, :])
 
+    def split_img(first):
+        split_rows(img, img_hi, img_lo, first, ROWS)
+
+    def split_txt(step):
+        for at in range(ROWS * step, ROWS * (step + 1), HALF):
+            high, low = split(txt[at:at + HALF, :])
+            txt_hi[at:at + HALF, :] = high
+            txt_lo[at:at + HALF, :] = low
+            both = at + ROWS * step
+            txt_both[both:both + HALF, :] = high
+            txt_both[both + ROWS:both + ROWS + HALF, :] = low
+
     def sigmoids(row, rows, col, cols):
         def one(at, count):
             a_hi, a_lo = img_hi[rows_at(at, count), :], img_lo[rows_at(at, count), :]
-            b_hi, b_lo = txt_hi[col:col + cols, :], txt_lo[col:col + cols, :]
-            dots = dot_nt(a_hi, b_hi) + (dot_nt(a_hi, b_lo) + dot_nt(a_lo, b_hi))
-            sig[rows_at(at, count), col:col + cols] = jax.nn.sigmoid(temper * dots + offset)
+            wide = cols - cols % 256
+            if wide:
+                b_hi, b_lo = txt_hi[col:col + wide, :], txt_lo[col:col + wide, :]
+                dots = dot_nt(a_hi, b_hi) + (dot_nt(a_hi, b_lo) + dot_nt(a_lo, b_hi))
+                sig[rows_at(at, count), col:col + wide] = jax.nn.sigmoid(temper * dots + offset)
+            if cols % 256:
+                last = col + wide
+                both = dot_nt(a_hi, txt_both[2 * last:2 * last + 2 * ROWS, :])
+                dots = both[:, :ROWS] + (both[:, ROWS:] + dot_nt(a_lo, txt_hi[last:last + ROWS, :]))
+                sig[rows_at(at, count), last:last + ROWS] = jax.nn.sigmoid(temper * dots + offset)
 
         if rows <= 256:
             one(row, rows)
@@ -158,11 +199,21 @@
             cs = slice(at, at + count)
             store(cs, dot_nn(l_hi, high[:, cs]) + (dot_nn(l_hi, low[:, cs]) + dot_nn(l_lo, high[:, cs])))
 
-    def image_grads(first, col=0, cols=4 * ROWS, add=False):
+    def image_grads(first, cols=4 * ROWS):
         def store(cs, value):
-            g_img[first:first + ROWS, cs] = g_img[first:first + ROWS, cs] + value if add else value
-
-        times(sig[first:first + ROWS, col:col + cols], txt_hi.at[col:col + cols], txt_lo.at[col:col + cols], store)
+            g_img[first:first + ROWS, cs] = value
+
+        times(sig[first:first + ROWS, 0:cols], txt_hi.at[0:cols], txt_lo.at[0:cols], store)
+
+    def add_image_grads(first, step):
+        s_hi, s_lo = split(sig[first:first + ROWS, ROWS * step:ROWS * (step + 1)])
+        s_hi = jnp.concatenate([s_hi, s_hi], axis=1)
+        for at, count in COLS:
+            cs = slice(at, at + count)
+            g_img[first:first + ROWS, cs] += (
+                dot_nn(s_hi, txt_both[2 * ROWS * step:2 * ROWS * (step + 1), cs])
+                + dot_nn(s_lo, txt_hi[ROWS * step:ROWS * (step + 1), cs])
+            )
 
     def text_grads(first, row=0, rows=8 * ROWS, add=False):
         def store(cs, value):
@@ -170,25 +221,33 @@
 
         times(sig[row:row + rows, first:first + ROWS].T, img_hi.at[row:row + rows], img_lo.at[row:row + rows], store)
 
+    for axis in ("x", "z"):
+        for side in (0, 1):
+            gather(axis, 1, side, 0)
+    normalize(1)
+    for axis in ("x", "z"):
+        for side in (0, 1):
+            gather(axis, 1, side, 1)
+    across(0)
+    for load in small:
+        load.wait()
+    meta[0, 0:4, :] = pos_ref[...]
+    meta[0, 4:5, :] = cnt_ref[...]
+    meta[0, 5:6, :] = row_ref[...]
+    meta[0, 6:8, :] = jnp.zeros((2, ROWS), jnp.int32)
     for slot, device in ((1, y_dev[0]), (2, y_dev[1]), (3, y_far)):
-        push(("m", slot), meta.at[0], meta.at[slot], device)
-    for part in (0, 1):
-        for axis in ("x", "z"):
-            for side in (0, 1):
-                gather(axis, 1, side, part)
-    across(0)
+        push("m", meta.at[0], meta.at[slot], device, LISTS)
     for step in (1, 2):
         for side in (0, 1):
             gather_y("yt", step, side)
 
-    split_rows(img, img_hi, img_lo, 0, ROWS)
-    split_rows(txt, txt_hi, txt_lo, 0, ROWS)
-    arrived(("c", 0))
-    split_rows(img, img_hi, img_lo, ROWS, ROWS)
+    split_img(0)
+    split_txt(0)
+    crossed(0)
+    split_img(ROWS)
     sigmoids(0, 256, 0, ROWS)
 
-    for slot in (1, 2, 3):
-        arrived(("m", slot))
+    arrived("m", meta.at[1:4])
     group_base = blk * (4 * ROWS)
     places = [lax.rem(grp + shift, 4) * ROWS + group_base for shift in (0, 3, 1, 2)]
     tall = lax.broadcasted_iota(jnp.int32, (ROWS, ROWS), 0)
@@ -213,7 +272,7 @@
 
     for axis in ("x", "z"):
         for side in (0, 1):
-            arrived((axis, 1, side, 0))
+            arrived((axis, 1, side, 0), piece(axis, 1, side, 0))
             gather(axis, 2, side, 0)
 
     own_ids, own_held = named(0), held(0)
@@ -224,79 +283,76 @@
 
     for axis in ("x", "z"):
         for side in (0, 1):
-            arrived((axis, 1, side, 1))
+            arrived((axis, 1, side, 1), piece(axis, 1, side, 1))
             gather(axis, 2, side, 1)
     across(1)
     for part in (0, 1):
         for axis in ("x", "z"):
             for side in (0, 1):
                 gather(axis, 3, side, part)
-    for side in (0, 1):
-        arrived(("yt", 1, side))
-        gather_y("yt", 3, side)
+    forward_y("yt")
     for step in (1, 2):
         for side in (0, 1):
             gather_y("yi", step, side)
 
-    split_rows(txt, txt_hi, txt_lo, ROWS, ROWS)
-    split_rows(img, img_hi, img_lo, 256, ROWS)
+    split_txt(1)
+    split_img(256)
     sigmoids(0, 256, ROWS, ROWS)
-    arrived(("c", 1))
-    split_rows(img, img_hi, img_lo, 256 + ROWS, ROWS)
-    sigmoids(256, 256, 0, 256)
-
-    for part in (0, 1):
-        for axis in ("x", "z"):
-            for side in (0, 1):
-                arrived((axis, 2, side, part))
+    sigmoids(256, ROWS, 0, 256)
+    crossed(1)
+    split_img(256 + ROWS)
+    sigmoids(256 + ROWS, ROWS, 0, 256)
+
+    gathered("x", 2)
     across(2)
-    split_rows(txt, txt_hi, txt_lo, 2 * ROWS, ROWS)
-    split_rows(img, img_hi, img_lo, 512, ROWS)
+    gathered("z", 2)
+    split_txt(2)
+    split_img(512)
     sigmoids(0, 512, 2 * ROWS, ROWS)
-    arrived(("c", 2))
-    split_rows(img, img_hi, img_lo, 512 + ROWS, ROWS)
-    sigmoids(512, 256, 0, 3 * ROWS)
+    sigmoids(512, ROWS, 0, 3 * ROWS)
+    crossed(2)
+    split_img(512 + ROWS)
+    sigmoids(512 + ROWS, ROWS, 0, 3 * ROWS)
+    image_grads(512 + ROWS, 3 * ROWS)
+    image_grads(512, 3 * ROWS)
     text_grads(2 * ROWS, 0, 768)
-    image_grads(512 + ROWS, 0, 3 * ROWS)
-    image_grads(512, 0, 3 * ROWS)
-
-    for part in (0, 1):
-        for side in (0, 1):
-            arrived(("x", 3, side, part))
+
+    gathered("x", 3)
     across(3)
-    for part in (0, 1):
-        for side in (0, 1):
-            arrived(("z", 3, side, part))
+    gathered("z", 3)
 
     def share(step):
         first = 2 * ROWS * step
-        push(("r", step), g_img.at[rows_at(first + ROWS, ROWS)], c_in.at[step], peer)
+        push(("r", step), g_img.at[rows_at(first + ROWS, ROWS)], c_in.at[step], peer, CORE)
 
     def joined(step):
         first = 2 * ROWS * step
-        arrived(("r", step))
+        arrived(("r", step), c_in.at[step])
         g_img[first:first + ROWS, :] += c_in[step]
 
     scatters = {"x": (g_img, 2 * ROWS, x_dev, x_in), "z": (g_txt, ROWS, z_dev, z_in)}
 
     def scatter(axis, turn):
         buffer, stride, devices, inbox = scatters[axis]
+        if turn == 2:
+            arrived((axis, "s", 0), inbox.at[0])
         for side in (0, 1):
             first = (2 * stride + side * HALF, stride + (1 - side) * HALF, 3 * stride + (1 - side) * HALF)[turn]
             if turn == 2:
-                arrived((axis, "s", 0, side))
-                buffer[first:first + HALF, :] += inbox[side, 0]
-            push((axis, "s", turn, side), buffer.at[rows_at(first, HALF)], inbox.at[side, turn], devices[side])
-
-    split_rows(txt, txt_hi, txt_lo, 3 * ROWS, ROWS)
-    sigmoids(512, 256, 3 * ROWS, ROWS)
-    image_grads(512 + ROWS, 3 * ROWS, ROWS, True)
+                buffer[first:first + HALF, :] += inbox[0, side]
+            push((axis, "s", turn), buffer.at[rows_at(first, HALF)], inbox.at[turn, side], devices[side], SCATTER)
+
+    split_txt(3)
+    sigmoids(512 + ROWS, ROWS, 3 * ROWS, ROWS)
+    add_image_grads(512 + ROWS, 3)
     share(2)
-    image_grads(512, 3 * ROWS, ROWS, True)
-    split_rows(img, img_hi, img_lo, 768, ROWS)
-    arrived(("c", 3))
-    split_rows(img, img_hi, img_lo, 768 + ROWS, ROWS)
-    sigmoids(768, 256, 2 * ROWS, ROWS)
+    sigmoids(512, ROWS, 3 * ROWS, ROWS)
+    add_image_grads(512, 3)
+    split_img(768)
+    sigmoids(768, ROWS, 2 * ROWS, ROWS)
+    crossed(3)
+    split_img(768 + ROWS)
+    sigmoids(768 + ROWS, ROWS, 2 * ROWS, ROWS)
     text_grads(2 * ROWS, 768, 256, True)
     scatter("z", 0)
     joined(2)
@@ -312,9 +368,7 @@
     text_grads(ROWS)
     scatter("z", 1)
 
-    for side in (0, 1):
-        arrived(("yi", 1, side))
-        gather_y("yi", 3, side)
+    forward_y("yi")
 
     sigmoids(768, 256, 3 * ROWS, ROWS)
     image_grads(768 + ROWS)
@@ -331,9 +385,7 @@
     image_grads(0)
     text_grads(0)
 
-    for side in (0, 1):
-        arrived(("yt", 2, side))
-        arrived(("yt", 3, side))
+    arrived(("yt", 2), y_txt.at[ROWS:3 * ROWS])
     split_rows(y_txt, yt_hi, yt_lo, 0, 3 * ROWS)
     own = rows_at(0, ROWS)
     dots = dot_nt(img_hi[own, :], yt_hi[...]) + (dot_nt(img_hi[own, :], yt_lo[...]) + dot_nt(img_lo[own, :], yt_hi[...]))
@@ -345,9 +397,7 @@
     times(coef, yt_hi, yt_lo, add_img)
     joined(0)
 
-    for side in (0, 1):
-        arrived(("yi", 2, side))
-        arrived(("yi", 3, side))
+    arrived(("yi", 2), y_img.at[ROWS:3 * ROWS])
     split_rows(y_img, yi_hi, yi_lo, 0, 3 * ROWS)
     dots = dot_nt(yi_hi[...], txt_hi[own, :]) + (dot_nt(yi_hi[...], txt_lo[own, :]) + dot_nt(yi_lo[...], txt_hi[own, :]))
     coef = mark_b[...] * (jax.nn.sigmoid(temper * dots + offset) - 1.0)
@@ -362,22 +412,24 @@
         ("z", g_txt, z_in, txt, norm_txt, gtxt_ref),
     )
     for axis, sums, inbox, unit, norm, out in ends:
+        arrived((axis, "s", 1), inbox.at[1])
         for side in (0, 1):
             at = slice((1 - side) * HALF, (2 - side) * HALF)
-            arrived((axis, "s", 1, side))
-            sums[at, :] += inbox[side, 1]
+            sums[at, :] += inbox[1, side]
     for axis, sums, inbox, unit, norm, out in ends:
-        for side in (0, 1):
-            arrived((axis, "s", 2, side))
+        arrived((axis, "s", 2), inbox.at[2])
         for half in (0, 1):
             at = slice(half * HALF, (half + 1) * HALF)
-            grad = temper * (sums[at, :] + inbox[half, 2])
+            grad = temper * (sums[at, :] + inbox[2, half])
             units = unit[at, :]
             along = jnp.sum(units * grad, axis=1, keepdims=True)
             out[at, :] = (grad - units * along) / norm[at, :]
 
-    for copy in copies.values():
-        copy.wait_send()
+    done(send_sem.at[CORE], g_img)
+    done(send_sem.at[GATHER], g_img.at[0:6 * ROWS])
+    done(send_sem.at[ALONG_Y], g_img.at[0:6 * ROWS])
+    done(send_sem.at[SCATTER], g_img.at[0:6 * ROWS])
+    done(send_sem.at[LISTS], meta.at[1:4])
 
 
 def hand_on(gimg_in, gtxt_in, gimg_out, gtxt_out, sems):
@@ -422,19 +474,20 @@
             pltpu.VMEM((3 * ROWS, D), BF16),
             pltpu.VMEM((3 * ROWS, D), BF16),
             pltpu.VMEM((3 * ROWS, D), BF16),
-            pltpu.VMEM((2, 3, HALF, D), F32),
-            pltpu.VMEM((2, 3, HALF, D), F32),
+            pltpu.VMEM((8 * ROWS, D), BF16),
+            pltpu.VMEM((3, 2, HALF, D), F32),
+            pltpu.VMEM((3, 2, HALF, D), F32),
             pltpu.VMEM((4, ROWS, D), F32),
             pltpu.VMEM((4, 8, ROWS), jnp.int32),
             pltpu.VMEM((ROWS, 4 * ROWS), F32),
             pltpu.VMEM((3 * ROWS, ROWS), F32),
             pltpu.VMEM((ROWS, 1), F32),
             pltpu.VMEM((ROWS, 1), F32),
-            pltpu.SemaphoreType.DMA((N_COPIES,)),
-            pltpu.SemaphoreType.DMA((N_COPIES,)),
+            pltpu.SemaphoreType.DMA((N_SEND,)),
+            pltpu.SemaphoreType.DMA((N_RECV,)),
         ],
         compiler_params=pltpu.CompilerParams(
-            collective_id=0, has_side_effects=True, vmem_limit_bytes=42 * 2**20
+            collective_id=0, has_side_effects=True, vmem_limit_bytes=46 * 2**20
         ),
         name="align_step",
     )(
@@ -451,7 +504,7 @@
     return pl.pallas_call(
         hand_on,
         out_shape=(rows, rows),
-        in_specs=[vmem, vmem],
+        in_specs=[anywhere, anywhere],
         out_specs=(anywhere, anywhere),
         scratch_shapes=[pltpu.SemaphoreType.DMA((2,))],
         name="hand_on",

time: 58.5 us -> 57.3 us (0.979)
  Pallas kernels: 55.6 us -> 54.5 us
    pallas_call x1, Pallas kernels: 54.6 us -> 53.4 us  [body(): pl.pallas_call(kernel, out_shape=(pltpu.VMEM((ROWS, D), F32), pltpu.VMEM(...]
where the time goes in v3:
time: 57.3 us; the launch traced here: 56.5 us
  Pallas kernels  54.5 us (95%)
  between operations  2.09 us (4%)
    pallas_call x1, Pallas kernels, body(): pl.pallas_call(kernel, out_shape=(pltpu.VMEM((ROWS, D), F32), pltpu.VMEM(...  53.4 us

profile of v3, /device:TPU:0, one launch (start us, length us, event | category | flops | bytes accessed | tf_op | source)
XLA Modules:
  0.0 56.5 jit_solution(6700040642946508723)
XLA Ops:
  1.9 53.4 %align_step.1 = (f32[128,1152]{1,0:T(8,128)S(1)}, f32[128,1152]{1,0:T(8,128)S(1)}) custom-call(f32[1]{0:T(128)S(6)} %copy.9.scale_ref, f32[1]{0:T(128)S(6)} %copy.10.bias_ref, f32[128,1152]{1,0:T(8,128)} %img_hbm.1, f32[128,1152]{1,0:T(8,128)} %txt_hbm.1, s32[4,128]{1,0:T(4,128)} %bitcast.3, s32[1,128]{1,0:T(1,128)} %bitcast.4, s32[1,128]{1,0:T(1,128)} %bitcast.5), custom_call_target="tpu_custom_call" | custom-call | tf_op jit(solution)/shard_map/align_step/pallas_call | solution.py:450
  55.4 1.0 %hand_on.1 = (f32[128,1152]{1,0:T(8,128)}, f32[128,1152]{1,0:T(8,128)}) custom-call(f32[128,1152]{1,0:T(8,128)S(1)} %get-tuple-element.4.gimg_in, f32[128,1152]{1,0:T(8,128)S(1)} %get-tuple-element.5.gtxt_in), custom_call_target="tpu_custom_call" | custom-call | tf_op jit(solution)/shard_map/hand_on/pallas_call | solution.py:504

commit v4 on v3

--- a/solution.py
+++ b/solution.py
@@ -13,7 +13,7 @@
 D = 1152
 COLS = ((0, 256), (256, 256), (512, 256), (768, 256), (1024, 128))
 N_SEND = 5
-N_RECV = 33
+N_RECV = 36
 CORE, GATHER, ALONG_Y, SCATTER, LISTS = range(N_SEND)
 F32 = jnp.float32
 BF16 = jnp.bfloat16
@@ -42,7 +42,7 @@
     img_ref, txt_ref, pos_ref, cnt_ref, row_ref, load_sem,
     img, txt, img_hi, img_lo, txt_hi, txt_lo, sig, g_img, g_txt,
     y_txt, y_img, yt_hi, yt_lo, yi_hi, yi_lo,
-    txt_both, x_in, z_in, c_in, meta, mark_a, mark_b, norm_img, norm_txt, send_sem, recv_sem,
+    txt_both, x_in, z_in, x_far, z_far, c_in, meta, mark_a, mark_b, norm_img, norm_txt, send_sem, recv_sem,
 ):
     blk, grp = lax.axis_index("blk"), lax.axis_index("grp")
     core = lax.rem(blk, 2)
@@ -67,20 +67,25 @@
     temper = scale_ref[0]
     offset = bias_ref[0]
     sources = ((img_hbm, img_ref, img, norm_img), (txt_hbm, txt_ref, txt, norm_txt))
-    for part in (0, 1):
+
+    def load(part):
         for hbm, ref, _, _ in sources:
             for half in (0, 1):
                 at = rows_at(half * HALF + part * PIECE, PIECE)
                 pltpu.make_async_copy(hbm.at[at], ref.at[at], load_sem.at[part]).start()
+
+    def loaded(part):
+        pltpu.make_async_copy(img_hbm, img_ref, load_sem.at[part]).wait()
+
+    load(0)
     small = [
         pltpu.make_async_copy(source, target, load_sem.at[2 + at])
         for at, (source, target) in enumerate(((pos_hbm, pos_ref), (cnt_hbm, cnt_ref), (row_hbm, row_ref)))
     ]
-    for load in small:
-        load.start()
+    for each in small:
+        each.start()
 
     def normalize(part):
-        pltpu.make_async_copy(img_hbm, img_ref, load_sem.at[part]).wait()
         for _, ref, unit, norm in sources:
             for half in (0, 1):
                 at = rows_at(half * HALF + part * PIECE, PIECE)
@@ -89,6 +94,8 @@
                 norm[at, :] = length
                 unit[at, :] = values / length
 
+    loaded(0)
+    load(1)
     normalize(0)
     pl.semaphore_wait(barrier, len(partners))
 
@@ -109,24 +116,34 @@
 
     rings = {"x": (img, 2 * ROWS, x_dev), "z": (txt, ROWS, z_dev)}
 
-    def piece(axis, step, side, part):
-        buffer, stride, _ = rings[axis]
-        return buffer.at[rows_at(stride * step + side * HALF + part * PIECE, PIECE)]
+    def place_of(axis, step, side, part):
+        stride = rings[axis][1]
+        if step == 3:
+            return 3 * stride + part * (stride // 2) + side * PIECE
+        return stride * step + side * HALF + part * PIECE
 
     def gather(axis, step, side, part):
         buffer, stride, devices = rings[axis]
-        first = {1: side * HALF, 2: stride + side * HALF, 3: (1 - side) * HALF}[step]
+        first = {1: side * HALF, 2: (1 - side) * HALF, 3: stride + side * HALF}[step]
         push(
-            (axis, 1, side, part) if step == 1 else (axis, step),
+            {1: (axis, 1, side), 2: (axis, 2), 3: (axis, 3, part)}[step],
             buffer.at[rows_at(first + part * PIECE, PIECE)],
-            piece(axis, step, side, part),
+            buffer.at[rows_at(place_of(axis, step, side, part), PIECE)],
             devices[side],
             GATHER,
         )
 
-    def gathered(axis, step):
+    def near(axis, side):
         buffer, stride, _ = rings[axis]
-        arrived((axis, step), buffer.at[rows_at(stride * step, ROWS)])
+        arrived((axis, 1, side), buffer.at[rows_at(stride + side * HALF, HALF)])
+
+    def near_rest(axis):
+        buffer, stride, _ = rings[axis]
+        arrived((axis, 2), buffer.at[rows_at(2 * stride, ROWS)])
+
+    def far(axis, part):
+        buffer, stride, _ = rings[axis]
+        arrived((axis, 3, part), buffer.at[rows_at(3 * stride + part * (stride // 2), HALF)])
 
     y_rings = {"yt": (txt, y_txt), "yi": (img, y_img)}
 
@@ -154,15 +171,22 @@
     def crossed(step):
         arrived(("c", step), img.at[rows_at(2 * ROWS * step + ROWS, ROWS)])
 
+    def across_far(part):
+        first = 6 * ROWS + part * ROWS
+        push(("c", 3, part), img.at[rows_at(first, HALF)], img.at[rows_at(first + HALF, HALF)], peer, CORE)
+
+    def crossed_far(part):
+        arrived(("c", 3, part), img.at[rows_at(6 * ROWS + part * ROWS + HALF, HALF)])
+
     def split_rows(source, high, low, first, count):
         for at in range(first, first + count, HALF):
             high[at:at + HALF, :], low[at:at + HALF, :] = split(source[at:at + HALF, :])
 
-    def split_img(first):
-        split_rows(img, img_hi, img_lo, first, ROWS)
-
-    def split_txt(step):
-        for at in range(ROWS * step, ROWS * (step + 1), HALF):
+    def split_img(first, count=ROWS):
+        split_rows(img, img_hi, img_lo, first, count)
+
+    def split_txt(step, first=0, count=ROWS):
+        for at in range(ROWS * step + first, ROWS * step + first + count, HALF):
             high, low = split(txt[at:at + HALF, :])
             txt_hi[at:at + HALF, :] = high
             txt_lo[at:at + HALF, :] = low
@@ -201,16 +225,16 @@
 
     def image_grads(first, cols=4 * ROWS):
         def store(cs, value):
-            g_img[first:first + ROWS, cs] = value
-
-        times(sig[first:first + ROWS, 0:cols], txt_hi.at[0:cols], txt_lo.at[0:cols], store)
-
-    def add_image_grads(first, step):
-        s_hi, s_lo = split(sig[first:first + ROWS, ROWS * step:ROWS * (step + 1)])
+            g_img[first:first + 2 * ROWS, cs] = value
+
+        times(sig[first:first + 2 * ROWS, 0:cols], txt_hi.at[0:cols], txt_lo.at[0:cols], store)
+
+    def add_image_grads(first, step, rows=ROWS):
+        s_hi, s_lo = split(sig[first:first + rows, ROWS * step:ROWS * (step + 1)])
         s_hi = jnp.concatenate([s_hi, s_hi], axis=1)
         for at, count in COLS:
             cs = slice(at, at + count)
-            g_img[first:first + ROWS, cs] += (
+            g_img[first:first + rows, cs] += (
                 dot_nn(s_hi, txt_both[2 * ROWS * step:2 * ROWS * (step + 1), cs])
                 + dot_nn(s_lo, txt_hi[ROWS * step:ROWS * (step + 1), cs])
             )
@@ -221,16 +245,29 @@
 
         times(sig[row:row + rows, first:first + ROWS].T, img_hi.at[row:row + rows], img_lo.at[row:row + rows], store)
 
+    def add_text_grads(first, row):
+        s_hi, s_lo = split(sig[row:row + ROWS, first:first + ROWS].T)
+        s_hi = jnp.concatenate([s_hi, s_hi], axis=1)
+        for at, count in COLS:
+            cs = slice(at, at + count)
+            both = jnp.concatenate([img_hi[row:row + ROWS, cs], img_lo[row:row + ROWS, cs]], axis=0)
+            g_txt[first:first + ROWS, cs] += dot_nn(s_hi, both) + dot_nn(s_lo, img_hi[row:row + ROWS, cs])
+
     for axis in ("x", "z"):
         for side in (0, 1):
             gather(axis, 1, side, 0)
+    loaded(1)
     normalize(1)
     for axis in ("x", "z"):
         for side in (0, 1):
             gather(axis, 1, side, 1)
+    for part in (0, 1):
+        for axis in ("x", "z"):
+            for side in (0, 1):
+                gather(axis, 2, side, part)
     across(0)
-    for load in small:
-        load.wait()
+    for each in small:
+        each.wait()
     meta[0, 0:4, :] = pos_ref[...]
     meta[0, 4:5, :] = cnt_ref[...]
     meta[0, 5:6, :] = row_ref[...]
@@ -270,11 +307,6 @@
         ]
         return jnp.concatenate(tiles, axis=1)
 
-    for axis in ("x", "z"):
-        for side in (0, 1):
-            arrived((axis, 1, side, 0), piece(axis, 1, side, 0))
-            gather(axis, 2, side, 0)
-
     own_ids, own_held = named(0), held(0)
     mark_a[:, 0:ROWS] = dot_nn(own_held, own_ids)
     for slot in (1, 2, 3):
@@ -283,13 +315,10 @@
 
     for axis in ("x", "z"):
         for side in (0, 1):
-            arrived((axis, 1, side, 1), piece(axis, 1, side, 1))
-            gather(axis, 2, side, 1)
+            near(axis, side)
+            for part in (0, 1):
+                gather(axis, 3, side, part)
     across(1)
-    for part in (0, 1):
-        for axis in ("x", "z"):
-            for side in (0, 1):
-                gather(axis, 3, side, part)
     forward_y("yt")
     for step in (1, 2):
         for side in (0, 1):
@@ -302,24 +331,31 @@
     crossed(1)
     split_img(256 + ROWS)
     sigmoids(256 + ROWS, ROWS, 0, 256)
-
-    gathered("x", 2)
+    image_grads(256, 2 * ROWS)
+    text_grads(ROWS, 0, 512)
+
+    near_rest("x")
     across(2)
-    gathered("z", 2)
+    near_rest("z")
     split_txt(2)
     split_img(512)
     sigmoids(0, 512, 2 * ROWS, ROWS)
+    add_image_grads(256, 2, 2 * ROWS)
     sigmoids(512, ROWS, 0, 3 * ROWS)
+    add_text_grads(ROWS, 512)
     crossed(2)
     split_img(512 + ROWS)
     sigmoids(512 + ROWS, ROWS, 0, 3 * ROWS)
-    image_grads(512 + ROWS, 3 * ROWS)
-    image_grads(512, 3 * ROWS)
-    text_grads(2 * ROWS, 0, 768)
-
-    gathered("x", 3)
-    across(3)
-    gathered("z", 3)
+    add_text_grads(ROWS, 512 + ROWS)
+
+    far("x", 0)
+    across_far(0)
+    far("z", 0)
+    split_txt(3, 0, HALF)
+    split_img(768, HALF)
+    far("x", 1)
+    across_far(1)
+    far("z", 1)
 
     def share(step):
         first = 2 * ROWS * step
@@ -330,60 +366,85 @@
         arrived(("r", step), c_in.at[step])
         g_img[first:first + ROWS, :] += c_in[step]
 
-    scatters = {"x": (g_img, 2 * ROWS, x_dev, x_in), "z": (g_txt, ROWS, z_dev, z_in)}
-
-    def scatter(axis, turn):
-        buffer, stride, devices, inbox = scatters[axis]
-        if turn == 2:
-            arrived((axis, "s", 0), inbox.at[0])
-        for side in (0, 1):
-            first = (2 * stride + side * HALF, stride + (1 - side) * HALF, 3 * stride + (1 - side) * HALF)[turn]
-            if turn == 2:
-                buffer[first:first + HALF, :] += inbox[0, side]
-            push((axis, "s", turn), buffer.at[rows_at(first, HALF)], inbox.at[turn, side], devices[side], SCATTER)
-
-    split_txt(3)
-    sigmoids(512 + ROWS, ROWS, 3 * ROWS, ROWS)
-    add_image_grads(512 + ROWS, 3)
+    def share_far(part):
+        first = 6 * ROWS + part * ROWS + HALF
+        push(("r", 3), g_img.at[rows_at(first, HALF)], c_in.at[3, rows_at(part * HALF, HALF)], peer, CORE)
+
+    def joined_far():
+        arrived(("r", 3), c_in.at[3])
+        for part in (0, 1):
+            first = 6 * ROWS + part * ROWS
+            g_img[first:first + HALF, :] += c_in[3, part * HALF:(part + 1) * HALF]
+
+    scatters = {"x": (g_img, 2 * ROWS, x_dev, x_in, x_far), "z": (g_txt, ROWS, z_dev, z_in, z_far)}
+
+    def scatter_near(axis):
+        buffer, stride, devices, inbox, _ = scatters[axis]
+        for side in (0, 1):
+            first = stride + (1 - side) * HALF
+            push((axis, "s", 1), buffer.at[rows_at(first, HALF)], inbox.at[0, side], devices[side], SCATTER)
+
+    def scatter_far(axis):
+        buffer, stride, devices, _, inbox = scatters[axis]
+        for part in (0, 1):
+            for side in (0, 1):
+                first = place_of(axis, 3, side, part)
+                push((axis, "s", 3, part), buffer.at[rows_at(first, PIECE)], inbox.at[part, side], devices[side], SCATTER)
+
+    def scatter_rest(axis, part):
+        buffer, stride, devices, inbox, relay = scatters[axis]
+        arrived((axis, "s", 3, part), relay.at[part])
+        for side in (0, 1):
+            first = 2 * stride + (1 - side) * HALF + part * PIECE
+            buffer[first:first + PIECE, :] += relay[part, side]
+            push(
+                (axis, "s", 2, part), buffer.at[rows_at(first, PIECE)], inbox.at[1 + part, side, rows_at(0, PIECE)],
+                devices[side], SCATTER,
+            )
+
+    split_txt(3, HALF, HALF)
+    sigmoids(256, 256, 3 * ROWS, ROWS)
+    add_image_grads(256 + ROWS, 3)
+    share(1)
+    add_image_grads(256, 3)
+    split_img(896, HALF)
+    crossed_far(0)
+    split_img(768 + HALF, HALF)
+    sigmoids(768, ROWS, ROWS, ROWS)
+    add_text_grads(ROWS, 768)
+    crossed_far(1)
+    split_img(896 + HALF, HALF)
+    sigmoids(896, ROWS, ROWS, ROWS)
+    add_text_grads(ROWS, 896)
+    scatter_near("z")
+    joined(1)
+    scatter_near("x")
+
+    sigmoids(768, 256, 0, ROWS)
+    sigmoids(768, 256, 2 * ROWS, 2 * ROWS)
+    image_grads(768)
+    share_far(0)
+    share_far(1)
+    sigmoids(0, 256, 3 * ROWS, ROWS)
+    sigmoids(512, 256, 3 * ROWS, ROWS)
+    text_grads(3 * ROWS)
+    scatter_far("z")
+    joined_far()
+    scatter_far("x")
+
+    forward_y("yi")
+
+    image_grads(512)
     share(2)
-    sigmoids(512, ROWS, 3 * ROWS, ROWS)
-    add_image_grads(512, 3)
-    split_img(768)
-    sigmoids(768, ROWS, 2 * ROWS, ROWS)
-    crossed(3)
-    split_img(768 + ROWS)
-    sigmoids(768 + ROWS, ROWS, 2 * ROWS, ROWS)
-    text_grads(2 * ROWS, 768, 256, True)
-    scatter("z", 0)
+    text_grads(2 * ROWS)
     joined(2)
-    scatter("x", 0)
-
-    sigmoids(0, 512, 3 * ROWS, ROWS)
-    image_grads(256 + ROWS)
-    share(1)
-    image_grads(256)
-    sigmoids(768, 256, 0, 2 * ROWS)
-    joined(1)
-    scatter("x", 1)
-    text_grads(ROWS)
-    scatter("z", 1)
-
-    forward_y("yi")
-
-    sigmoids(768, 256, 3 * ROWS, ROWS)
-    image_grads(768 + ROWS)
-    share(3)
-    image_grads(768)
-    text_grads(3 * ROWS)
-    joined(3)
-    scatter("x", 2)
-    scatter("z", 2)
-
-    image_grads(ROWS)
-    share(0)
+
     sig[0:ROWS, 0:ROWS] -= mark_a[:, 0:ROWS]
     image_grads(0)
+    share(0)
     text_grads(0)
+    scatter_rest("x", 0)
+    scatter_rest("z", 0)
 
     arrived(("yt", 2), y_txt.at[ROWS:3 * ROWS])
     split_rows(y_txt, yt_hi, yt_lo, 0, 3 * ROWS)
@@ -395,6 +456,8 @@
         g_img[0:ROWS, cs] += value
 
     times(coef, yt_hi, yt_lo, add_img)
+    scatter_rest("x", 1)
+    scatter_rest("z", 1)
     joined(0)
 
     arrived(("yi", 2), y_img.at[ROWS:3 * ROWS])
@@ -412,18 +475,19 @@
         ("z", g_txt, z_in, txt, norm_txt, gtxt_ref),
     )
     for axis, sums, inbox, unit, norm, out in ends:
-        arrived((axis, "s", 1), inbox.at[1])
+        arrived((axis, "s", 1), inbox.at[0])
         for side in (0, 1):
             at = slice((1 - side) * HALF, (2 - side) * HALF)
-            sums[at, :] += inbox[1, side]
-    for axis, sums, inbox, unit, norm, out in ends:
-        arrived((axis, "s", 2), inbox.at[2])
-        for half in (0, 1):
-            at = slice(half * HALF, (half + 1) * HALF)
-            grad = temper * (sums[at, :] + inbox[2, half])
-            units = unit[at, :]
-            along = jnp.sum(units * grad, axis=1, keepdims=True)
-            out[at, :] = (grad - units * along) / norm[at, :]
+            sums[at, :] += inbox[0, side]
+    for part in (0, 1):
+        for axis, sums, inbox, unit, norm, out in ends:
+            arrived((axis, "s", 2, part), inbox.at[1 + part, :, rows_at(0, PIECE)])
+            for half in (0, 1):
+                at = slice(half * HALF + part * PIECE, half * HALF + (part + 1) * PIECE)
+                grad = temper * (sums[at, :] + inbox[1 + part, half, 0:PIECE])
+                units = unit[at, :]
+                along = jnp.sum(units * grad, axis=1, keepdims=True)
+                out[at, :] = (grad - units * along) / norm[at, :]
 
     done(send_sem.at[CORE], g_img)
     done(send_sem.at[GATHER], g_img.at[0:6 * ROWS])
@@ -477,6 +541,8 @@
             pltpu.VMEM((8 * ROWS, D), BF16),
             pltpu.VMEM((3, 2, HALF, D), F32),
             pltpu.VMEM((3, 2, HALF, D), F32),
+            pltpu.VMEM((2, 2, PIECE, D), F32),
+            pltpu.VMEM((2, 2, PIECE, D), F32),
             pltpu.VMEM((4, ROWS, D), F32),
             pltpu.VMEM((4, 8, ROWS), jnp.int32),
             pltpu.VMEM((ROWS, 4 * ROWS), F32),

time: 57.3 us -> 56.8 us (level)
  no operation moved by 1% of the time
where the time goes in v4:
time: 56.8 us; the launch traced here: 56.4 us
  Pallas kernels  54.3 us (96%)
  between operations  2.11 us (4%)
    pallas_call x1, Pallas kernels, body(): pl.pallas_call(kernel, out_shape=(pltpu.VMEM((ROWS, D), F32), pltpu.VMEM(...  53.3 us

profile of v4, /device:TPU:0, one launch (start us, length us, event | category | flops | bytes accessed | tf_op | source)
XLA Modules:
  0.0 56.4 jit_solution(11658995084028523355)
XLA Ops:
  1.9 53.3 %align_step.1 = (f32[128,1152]{1,0:T(8,128)S(1)}, f32[128,1152]{1,0:T(8,128)S(1)}) custom-call(f32[1]{0:T(128)S(6)} %copy.9.scale_ref, f32[1]{0:T(128)S(6)} %copy.10.bias_ref, f32[128,1152]{1,0:T(8,128)} %img_hbm.1, f32[128,1152]{1,0:T(8,128)} %txt_hbm.1, s32[4,128]{1,0:T(4,128)} %bitcast.3, s32[1,128]{1,0:T(1,128)} %bitcast.4, s32[1,128]{1,0:T(1,128)} %bitcast.5), custom_call_target="tpu_custom_call" | custom-call | tf_op jit(solution)/shard_map/align_step/pallas_call | solution.py:514
  55.2 1.0 %hand_on.1 = (f32[128,1152]{1,0:T(8,128)}, f32[128,1152]{1,0:T(8,128)}) custom-call(f32[128,1152]{1,0:T(8,128)S(1)} %get-tuple-element.4.gimg_in, f32[128,1152]{1,0:T(8,128)S(1)} %get-tuple-element.5.gtxt_in), custom_call_target="tpu_custom_call" | custom-call | tf_op jit(solution)/shard_map/hand_on/pallas_call | solution.py:570

commit v5 on v4

--- a/solution.py
+++ b/solution.py
@@ -407,6 +407,12 @@
     add_image_grads(256 + ROWS, 3)
     share(1)
     add_image_grads(256, 3)
+
+    @pl.when(core == 0)
+    def _():
+        joined(1)
+        scatter_near("x")
+
     split_img(896, HALF)
     crossed_far(0)
     split_img(768 + HALF, HALF)
@@ -417,8 +423,10 @@
     sigmoids(896, ROWS, ROWS, ROWS)
     add_text_grads(ROWS, 896)
     scatter_near("z")
-    joined(1)
-    scatter_near("x")
+    @pl.when(core == 1)
+    def _():
+        joined(1)
+        scatter_near("x")
 
     sigmoids(768, 256, 0, ROWS)
     sigmoids(768, 256, 2 * ROWS, 2 * ROWS)

time: 56.8 us -> 56.5 us (level)
  Pallas kernels: 54.3 us -> 53.7 us
    pallas_call x1, Pallas kernels: 53.3 us -> 52.7 us  [body(): pl.pallas_call(kernel, out_shape=(pltpu.VMEM((ROWS, D), F32), pltpu.VMEM(...]
where the time goes in v5:
time: 56.5 us; the launch traced here: 55.8 us
  Pallas kernels  53.7 us (95%)
  between operations  2.09 us (4%)
    pallas_call x1, Pallas kernels, body(): pl.pallas_call(kernel, out_shape=(pltpu.VMEM((ROWS, D), F32), pltpu.VMEM(...  52.7 us

profile of v5, /device:TPU:0, one launch (start us, length us, event | category | flops | bytes accessed | tf_op | source)
XLA Modules:
  0.0 55.8 jit_solution(1430667449469354523)
XLA Ops:
  1.9 52.7 %align_step.1 = (f32[128,1152]{1,0:T(8,128)S(1)}, f32[128,1152]{1,0:T(8,128)S(1)}) custom-call(f32[1]{0:T(128)S(6)} %copy.9.scale_ref, f32[1]{0:T(128)S(6)} %copy.10.bias_ref, f32[128,1152]{1,0:T(8,128)} %img_hbm.1, f32[128,1152]{1,0:T(8,128)} %txt_hbm.1, s32[4,128]{1,0:T(4,128)} %bitcast.3, s32[1,128]{1,0:T(1,128)} %bitcast.4, s32[1,128]{1,0:T(1,128)} %bitcast.5), custom_call_target="tpu_custom_call" | custom-call | tf_op jit(solution)/shard_map/align_step/pallas_call | solution.py:522
  54.6 1.0 %hand_on.1 = (f32[128,1152]{1,0:T(8,128)}, f32[128,1152]{1,0:T(8,128)}) custom-call(f32[128,1152]{1,0:T(8,128)S(1)} %get-tuple-element.4.gimg_in, f32[128,1152]{1,0:T(8,128)S(1)} %get-tuple-element.5.gtxt_in), custom_call_target="tpu_custom_call" | custom-call | tf_op jit(solution)/shard_map/hand_on/pallas_call | solution.py:578

commit v6 on v5

--- a/solution.py
+++ b/solution.py
@@ -318,7 +318,8 @@
             near(axis, side)
             for part in (0, 1):
                 gather(axis, 3, side, part)
-    across(1)
+        if axis == "x":
+            across(1)
     forward_y("yt")
     for step in (1, 2):
         for side in (0, 1):
@@ -445,12 +446,11 @@
     image_grads(512)
     share(2)
     text_grads(2 * ROWS)
-    joined(2)
-
     sig[0:ROWS, 0:ROWS] -= mark_a[:, 0:ROWS]
     image_grads(0)
     share(0)
     text_grads(0)
+    joined(2)
     scatter_rest("x", 0)
     scatter_rest("z", 0)
 

time: 56.5 us -> 56.5 us (level)
  no operation moved by 1% of the time
where the time goes in v6:
time: 56.5 us; the launch traced here: 55.8 us
  Pallas kernels  53.7 us (95%)
  between operations  2.09 us (4%)
    pallas_call x1, Pallas kernels, body(): pl.pallas_call(kernel, out_shape=(pltpu.VMEM((ROWS, D), F32), pltpu.VMEM(...  52.7 us

profile of v6, /device:TPU:0, one launch (start us, length us, event | category | flops | bytes accessed | tf_op | source)
XLA Modules:
  0.0 55.8 jit_solution(6627782934834998490)
XLA Ops:
  1.9 52.7 %align_step.1 = (f32[128,1152]{1,0:T(8,128)S(1)}, f32[128,1152]{1,0:T(8,128)S(1)}) custom-call(f32[1]{0:T(128)S(6)} %copy.9.scale_ref, f32[1]{0:T(128)S(6)} %copy.10.bias_ref, f32[128,1152]{1,0:T(8,128)} %img_hbm.1, f32[128,1152]{1,0:T(8,128)} %txt_hbm.1, s32[4,128]{1,0:T(4,128)} %bitcast.3, s32[1,128]{1,0:T(1,128)} %bitcast.4, s32[1,128]{1,0:T(1,128)} %bitcast.5), custom_call_target="tpu_custom_call" | custom-call | tf_op jit(solution)/shard_map/align_step/pallas_call | solution.py:522
  54.6 1.0 %hand_on.1 = (f32[128,1152]{1,0:T(8,128)}, f32[128,1152]{1,0:T(8,128)}) custom-call(f32[128,1152]{1,0:T(8,128)S(1)} %get-tuple-element.4.gimg_in, f32[128,1152]{1,0:T(8,128)S(1)} %get-tuple-element.5.gtxt_in), custom_call_target="tpu_custom_call" | custom-call | tf_op jit(solution)/shard_map/hand_on/pallas_call | solution.py:578
